TPU v7x, 256 devices: a whole 4x4x8 slice. The times are simulated.
256 devices in a mesh: tok: 32 (over z, y), voc: 8 (over x, core).
Axes of the slice: x: 4, y: 4, z: 8, core: 2. Of those that a mesh axis runs over, the one named last changes fastest.
Arguments:
- student_hidden: bfloat16 [2048, 2048], P('tok'), may hold values from -7.5 to 7.5
- learner_projection_weights: bfloat16 [2048, 131072], P(None, ('voc', 'tok')), may hold values from -0.41984465 to 0.41984465
- mentor_unscaled_scores: bfloat16 [2048, 131072], P('tok', 'voc'), may hold values from -20 to 480
- token_teacher_row: int32 [2048], replicated, may hold values from 0 to 2047, as said below
- sequence_length_list: int32 [8], replicated, may hold values from 1 to 512, 2048 in all
Outputs:
- distill_objective: float32 [], replicated
- grad_hidden: bfloat16 [2048, 2048], P(('tok', 'voc'))
- grad_weight: bfloat16 [2048, 131072], P(None, ('voc', 'tok'))
Inputs may be any that keep to these rules, and one draw needn't show every extreme that they name: student token s takes the teacher's row token_teacher_row[s]; every row is taken once. `sequence_length_list`: the 8 sequences fill all 2048 tokens.
All inputs are finite; a program needn't handle non-finite values.
Results may differ from a plain program's by a relative error of at most 0.007.
Values may be sent and summed in bfloat16 or wider, within the bound.
A program may use at most 128 MiB of HBM per device.

v0:
```python
import jax
import jax.numpy as jnp
from jax import lax
from jax.sharding import PartitionSpec as P

smoothing_divisor = 2.0
objective_scaling = 512.0


def token_valid(sequence_length_list, total):
    ends = jnp.cumsum(sequence_length_list) - 1
    places = jnp.arange(total, dtype=jnp.int32)
    hits = jnp.sum((places[:, None] == ends[None, :]).astype(jnp.float32), axis=1)
    return 1.0 - hits


def body(
    student_hidden,
    learner_projection_weights,
    mentor_unscaled_scores,
    token_teacher_row,
    sequence_length_list,
):
    teacher_columns = lax.all_to_all(
        mentor_unscaled_scores, "tok", split_axis=1, concat_axis=0, tiled=True
    )
    hidden_gathered = lax.all_gather(student_hidden, "tok", axis=0, tiled=True)
    row_count_total = hidden_gathered.shape[0]
    learner_scores = (
        jnp.dot(hidden_gathered, learner_projection_weights, preferred_element_type=jnp.float32)
        / smoothing_divisor
    )
    mentor_reordered_scores = (
        jnp.take(teacher_columns, token_teacher_row, axis=0).astype(jnp.float32) / smoothing_divisor
    )
    local_student = jnp.max(learner_scores, axis=1)
    local_teacher = jnp.max(mentor_reordered_scores, axis=1)
    top_student, top_teacher = lax.pmax((local_student, local_teacher), ("tok", "voc"))
    exp_student = jnp.exp(learner_scores - top_student[:, None])
    exp_teacher = jnp.exp(mentor_reordered_scores - top_teacher[:, None])
    sum_student, sum_teacher, cross = lax.psum(
        (
            jnp.sum(exp_student, axis=1),
            jnp.sum(exp_teacher, axis=1),
            jnp.sum(exp_teacher * (mentor_reordered_scores - learner_scores), axis=1),
        ),
        ("tok", "voc"),
    )
    learner_distribution = exp_student / sum_student[:, None]
    mentor_distribution = exp_teacher / sum_teacher[:, None]
    log_total_student = top_student + jnp.log(sum_student)
    log_total_teacher = top_teacher + jnp.log(sum_teacher)
    kullback_leibler_term = cross / sum_teacher - log_total_teacher + log_total_student
    usable_indicator = token_valid(sequence_length_list, row_count_total)
    distill_objective = (
        smoothing_divisor
        * smoothing_divisor
        * jnp.sum(usable_indicator * kullback_leibler_term)
        / (row_count_total - sequence_length_list.shape[0])
    )
    derivative_routine = (
        objective_scaling
        * smoothing_divisor
        * usable_indicator[:, None]
        * (learner_distribution - mentor_distribution)
    ).astype(jnp.bfloat16)
    grad_weight = lax.dot_general(
        hidden_gathered,
        derivative_routine,
        (((0,), (0,)), ((), ())),
        preferred_element_type=jnp.float32,
    ).astype(jnp.bfloat16)
    grad_hidden = lax.psum_scatter(
        lax.dot_general(
            derivative_routine,
            learner_projection_weights,
            (((1,), (1,)), ((), ())),
            preferred_element_type=jnp.float32,
        ),
        ("tok", "voc"),
        scatter_dimension=0,
        tiled=True,
    )
    return (distill_objective, grad_hidden.astype(jnp.bfloat16), grad_weight)


def solution(mesh):
    placed = (P("tok", None), P(None, ("voc", "tok")), P("tok", "voc"), P(), P())
    return jax.shard_map(
        body,
        mesh=mesh,
        in_specs=placed,
        out_specs=(P(), P(("tok", "voc"), None), P(None, ("voc", "tok"))),
        check_vma=False,
    )
```

profile of v0, /device:TPU:1, one launch (start us, length us, event | category | flops | bytes accessed | tf_op | source)
XLA Modules:
  0.0 1647.0 jit_solution(566593328342142146)
XLA Ops:
  7.2 0.0 copy-start
  7.2 0.0 all-gather.2.cloned.1.call-start
  7.2 0.7 all-gather.2.cloned.1.call-update
  7.9 0.0 copy-start.2
  7.9 0.0 copy-start.1
  7.9 3.2 copy.16
  11.1 12.2 all-to-all-start
  23.3 0.0 reduce-scatter.2.cloned.1.call-start
  23.4 0.0 copy-done.2
  23.4 0.2 reduce-window.8
  23.6 0.1 convert_reduce_fusion
  23.7 0.0 copy-done.1
  23.7 57.9 %all-to-all-done = bf16[64,32,512]{2,0,1:T(8,128)(2,1)} async-done(((bf16[64,32,512]{2,0,1:T(8,128)(2,1)}), bf16[64,32,512]{2,0,1:T(8,128)(2,1)}, u32[]{:S(2)}, u32[]{:S(2)}) %all-to-all-start) | async-done | bytes 2097184 | tf_op jit(solution)/shard_map/all_to_all | solution.py:24
  81.6 11.5 gather_fusion
  93.1 4.0 copy.12
  97.1 2.3 fusion.1
  99.4 78.0 %pmax.14 = f32[2048]{0:T(1024)S(1)} all-reduce(f32[2048]{0:T(1024)S(1)} %fusion.1), channel_id=1, replica_groups=mesh['tok'=32,'voc'=8] {'tok','voc'}, use_global_device_ids=true, to_apply=%region_3.4 | all-reduce | flops 2048 | bytes 16384 | tf_op jit(solution)/shard_map/pmax | solution.py:38
  177.5 0.0 all-gather.2.cloned.1.call-done
  177.5 0.0 copy-done
  177.5 11.0 multiply_reduce_fusion
  188.5 73.4 %pmax.15 = f32[2048]{0:T(1024)S(1)} all-reduce(f32[2048]{0:T(1024)S(1)} %get-tuple-element.10), channel_id=1, replica_groups=mesh['tok'=32,'voc'=8] {'tok','voc'}, use_global_device_ids=true, to_apply=%region_9.10 | all-reduce | flops 2048 | bytes 16384 | tf_op jit(solution)/shard_map/pmax | solution.py:38
  261.9 2.9 fusion.2
  264.8 73.2 %all-reduce = (f32[2048]{0:T(1024)S(1)}, f32[2048]{0:T(1024)S(1)}, f32[2048]{0:T(1024)S(1)}) all-reduce(f32[2048]{0:T(1024)S(1)} %fusion.2, f32[2048]{0:T(1024)S(1)} %get-tuple-element.11, f32[2048]{0:T(1024)S(1)} %get-tuple-element.9), channel_id=1, replica_groups=mesh['tok'=32,'voc'=8] {'tok','voc'}, use_global_device_ids=true, to_apply=%region_11.12 | all-reduce | flops 6144 | bytes 49152 | tf_op jit(solution)/shard_map/psum | solution.py:41
  338.0 0.6 subtract_multiply_fusion
  338.6 14.1 fusion.5
  352.7 0.0 reduce-scatter.2.cloned.1.call-update
  352.8 12.0 fusion.3
  364.8 3.9 copy.13
  369.4 1268.2 %reduce-scatter.2.cloned.1.call-done = f32[8,2048]{1,0:T(8,128)} async-done(((f32[2048,2048]{1,0:T(8,128)}), f32[8,2048]{1,0:T(8,128)}) %reduce-scatter.2.cloned.1.call-update) | async-done | bytes 65552 | tf_op jit(solution)/shard_map/reduce_scatter | solution.py:73
  1637.5 1.5 convert_element_type.21
  (3 shorter events, 0.0 us)
Async XLA Ops:
  7.2 170.3 %copy-start = (bf16[2048,512]{1,0:T(8,128)(2,1)S(1)}, bf16[2048,512]{1,0:T(8,128)(2,1)}, u32[]{:S(2)}) copy-start(bf16[2048,512]{1,0:T(8,128)(2,1)} %param.6) | copy-start | bytes 6291460
  7.2 170.3 %all-gather.2.cloned.1.call-start = ((), (), s32[]{:S(2)}) async-start(), calls=%async_computation.2 | async-start | bytes 8650752 | tf_op jit(solution)/shard_map/all_gather | solution.py:27
  7.9 15.4 copy-start.2
  7.9 15.7 copy-start.1
  11.1 70.5 %all-to-all-start = ((bf16[64,32,512]{2,0,1:T(8,128)(2,1)}), bf16[64,32,512]{2,0,1:T(8,128)(2,1)}, u32[]{:S(2)}, u32[]{:S(2)}) async-start(bf16[64,32,512]{2,0,1:T(8,128)(2,1)} %bitcast.16), calls=%async_computation | async-start | bytes 4194304 | tf_op jit(solution)/shard_map/all_to_all | solution.py:24
  23.3 1614.2 %reduce-scatter.2.cloned.1.call-start = ((), (), s32[]{:S(2)}) async-start(), calls=%async_computation.3 | async-start | bytes 16842752 | tf_op jit(solution)/shard_map/reduce_scatter | solution.py:73
Sparse Core Ops, SparseCore 0:
  10.6 119.5 all-gather.1
  352.9 1284.5 reduce-scatter.1
where the time goes:
time: 1650 us
  waiting for transfers between devices  1330 us (81%)
  blocking collectives  225 us (14%)
  matrix products  37.1 us (2%)
  local copies, waits for them, and re-layouts  22.6 us (1%)
    reduce_scatter x1, waiting for transfers between devices, body(): lax.psum_scatter(lax.dot_general(derivative_routine, learner_projection_w...  1270 us
    pmax x2, blocking collectives, body(): lax.pmax((local_student, local_teacher), ('tok', 'voc'))  151 us
    psum x1, blocking collectives, body(): lax.psum((jnp.sum(exp_student, axis=1), jnp.sum(exp_teacher, axis=1), jnp...  73.2 us
    all_to_all x1, waiting for transfers between devices, body(): lax.all_to_all(mentor_unscaled_scores, 'tok', split_axis=1, concat_axis=0...  57.9 us
  transfers between devices with their start and end apart: 3, of which 2 were waited for; matrix products, arithmetic and copies ran while one was open for 2% of the time, Pallas kernels for 0%

commit v1 on v0

v1 whole, which is shorter than its diff:
```python
import functools

import jax
import jax.numpy as jnp
from jax import lax
from jax.experimental import pallas as pl
from jax.experimental.pallas import tpu as pltpu
from jax.sharding import PartitionSpec as P

MESH = pl.DeviceIdType.MESH
F32 = jnp.float32
BF16 = jnp.bfloat16
TEMPERATURE = 2.0
SCALE = 512.0
LANES = 128


def mod(a, n):
    return lax.rem(a, n)


def kernel(
    dims,
    hidden,
    weights,
    mentor,
    rows,
    lengths,
    loss_out,
    grad_hidden,
    grad_weight,
    gathered,
    teacher,
    picks,
    scores,
    slope,
    mate_send,
    mate_recv,
    own_half,
    folded,
    first_a,
    first_b,
    second_a,
    second_b,
    got_a,
    got_b,
    last,
    final,
    final_recv,
    stat_voc,
    stat_y,
    stat_z,
    loss_voc,
    loss_y,
    loss_z,
    local_sem,
    s1_sem,
    t_sem,
    s2a_sem,
    s2b_sem,
    s3a_sem,
    s3b_sem,
    ca_sem,
    cb_sem,
    stat_voc_sem,
    stat_y_sem,
    stat_z_sem,
    loss_voc_sem,
    loss_y_sem,
    loss_z_sem,
    mate_sem,
    r1a_sem,
    r1b_sem,
    r2a_sem,
    r2b_sem,
    r3_sem,
    final_sem,
):
    Z, Y, X, R, V, D = dims
    tok, voc = lax.axis_index("tok"), lax.axis_index("voc")
    z, y = tok // Y, mod(tok, Y)
    x, core = voc // 2, mod(voc, 2)
    NT, NV = Z * Y, X * 2
    CH = Y * R
    N = Z * CH
    HALF = D // 2
    QUARTER = D // 4
    CS = D // NV
    CP = CS // 2
    nb = max(1, CH // LANES)
    q = CH // nb

    def at(dz=0, dy=0, dx=0, dc=0):
        return (
            mod(z + dz, Z) * Y + mod(y + dy, Y),
            mod(x + dx, X) * 2 + mod(core + dc, 2),
        )

    def copy(src, dst, sems, index, device):
        return pltpu.make_async_remote_copy(
            src_ref=src,
            dst_ref=dst,
            send_sem=sems.at[0, index],
            recv_sem=sems.at[1, index],
            device_id=device,
            device_id_type=MESH,
        )

    def each(n, body, start=0):
        def step(i, carry):
            body(i)
            return carry

        lax.fori_loop(start, n, step, 0)

    barrier = pltpu.get_barrier_semaphore()

    def greet_tok(i):
        pl.semaphore_signal(barrier, inc=1, device_id=at(dz=i // Y, dy=mod(i, Y)), device_id_type=MESH)

    def greet_voc(i):
        pl.semaphore_signal(barrier, inc=1, device_id=at(dx=i // 2, dc=mod(i, 2)), device_id_type=MESH)

    each(NT, greet_tok, 1)
    each(NV, greet_voc, 1)
    pl.semaphore_wait(barrier, NT - 1 + NV - 1)

    def s1(i):
        return copy(
            hidden.at[:, pl.ds(pl.multiple_of(voc * CS, CS), CS)],
            gathered.at[x, core, z, y],
            s1_sem,
            i,
            at(dz=i),
        )

    each(Z, lambda i: s1(i).start(), 1)
    own_columns = pltpu.make_async_copy(
        hidden.at[:, pl.ds(pl.multiple_of(voc * CS, CS), CS)],
        gathered.at[x, core, z, y],
        local_sem.at[0],
    )
    own_columns.start()

    def t_copy(i):
        device = at(dz=i // Y, dy=mod(i, Y))
        return copy(
            mentor.at[:, pl.ds(pl.multiple_of(device[0] * V, V), V)],
            teacher.at[pl.ds(pl.multiple_of(tok * R, R), R), :],
            t_sem,
            i,
            device,
        )

    each(NT, lambda i: t_copy(i).start(), 1)
    own_block = pltpu.make_async_copy(
        mentor.at[:, pl.ds(pl.multiple_of(tok * V, V), V)],
        teacher.at[pl.ds(pl.multiple_of(tok * R, R), R), :],
        local_sem.at[1],
    )
    own_block.start()

    eye = lax.broadcasted_iota(jnp.int32, (q, LANES), 0) == lax.broadcasted_iota(
        jnp.int32, (q, LANES), 1
    )
    eye_rows = lax.broadcasted_iota(jnp.int32, (R, LANES), 0) == lax.broadcasted_iota(
        jnp.int32, (R, LANES), 1
    )

    def columns_of(i):
        return mentor[:, pl.ds(pl.multiple_of(i * V, V), V)].astype(F32) / TEMPERATURE

    def fold(op, value):
        total = value[:, :LANES]
        for j in range(1, V // LANES):
            total = op(total, value[:, j * LANES : (j + 1) * LANES])
        return total

    top_t = lax.fori_loop(
        0,
        NT,
        lambda i, m: jnp.maximum(m, fold(jnp.maximum, columns_of(i))),
        jnp.full((R, LANES), -jnp.inf, F32),
    )
    top_t = jnp.max(top_t, axis=1, keepdims=True)
    sum_t = lax.fori_loop(
        0,
        NT,
        lambda i, s: s + fold(jnp.add, jnp.exp(columns_of(i) - top_t)),
        jnp.zeros((R, LANES), F32),
    )
    sum_t = jnp.sum(sum_t, axis=1, keepdims=True)

    def to_lanes(column, mask):
        return jnp.sum(jnp.where(mask, column, 0.0), axis=0, keepdims=True)

    stat_voc[voc, Z] = jnp.concatenate(
        [to_lanes(top_t, eye_rows), to_lanes(sum_t, eye_rows), jnp.zeros((6, LANES), F32)], axis=0
    )

    def fill_picks(k):
        here = pl.ds(pl.multiple_of(k * CH, CH), CH)
        wanted = rows[here, :]
        places = lax.broadcasted_iota(jnp.int32, (CH, N), 1)
        picks[here, :] = jnp.where(places == wanted, 1.0, 0.0).astype(BF16)

    each(Z, fill_picks)

    own_columns.wait()
    each(Z, lambda i: s1(i).wait(), 1)
    first, second = pl.ds(0, CP), pl.ds(CP, CP)

    def s2a(i):
        block = gathered.at[x, core, :, y, :, first]
        return copy(block, block, s2a_sem, i, at(dy=i))

    def s2b(i):
        block = gathered.at[x, core, :, y, :, second]
        return copy(block, block, s2b_sem, i, at(dx=i))

    each(Y, lambda i: s2a(i).start(), 1)
    each(X, lambda i: s2b(i).start(), 1)

    def s3a(i):
        block = gathered.at[x, core, :, :, :, first]
        return copy(block, block, s3a_sem, i, at(dx=i))

    def s3b(i):
        block = gathered.at[:, core, :, y, :, second]
        return copy(block, block, s3b_sem, i, at(dy=i))

    def ca(i):
        block = gathered.at[mod(x + X - i, X), core, :, :, :, first]
        return copy(block, block, ca_sem, i, at(dc=1))

    def cb(i):
        block = gathered.at[:, core, :, mod(y + Y - i, Y), :, second]
        return copy(block, block, cb_sem, i, at(dc=1))

    each(Y, lambda i: s2a(i).wait(), 1)
    each(X, lambda i: s3a(i).start(), 1)
    each(X, lambda i: s2b(i).wait(), 1)
    each(Y, lambda i: s3b(i).start(), 1)
    ca(0).start()
    cb(0).start()

    def on_x(i):
        s3a(i).wait()
        ca(i).start()

    def on_y(i):
        s3b(i).wait()
        cb(i).start()

    each(X, on_x, 1)
    each(Y, on_y, 1)
    each(X, lambda i: ca(i).wait())
    each(Y, lambda i: cb(i).wait())

    def hidden_of(b, k):
        return gathered[b // 2, b % 2, k].reshape(CH, CS)

    def score(k):
        here = pl.ds(pl.multiple_of(k * CH, CH), CH)
        wide = jnp.concatenate([hidden_of(b, k) for b in range(NV)], axis=1)
        value = jnp.dot(wide, weights[...], preferred_element_type=F32) / TEMPERATURE
        scores[here, :] = value
        top = jnp.max(value, axis=1, keepdims=True)
        total = jnp.sum(jnp.exp(value - top), axis=1, keepdims=True)
        parts = [to_lanes(top[j * q : (j + 1) * q], eye) for j in range(nb)]
        parts += [to_lanes(total[j * q : (j + 1) * q], eye) for j in range(nb)]
        parts.append(jnp.zeros((8 - 2 * nb, LANES), F32))
        stat_voc[voc, k] = jnp.concatenate(parts, axis=0)

    each(Z, score)

    def stage(buf, sems, slot, n, target, count=None):
        def c(i):
            block = buf.at[slot] if count is None else buf.at[slot, pl.ds(0, count)]
            return copy(block, block, sems, i, target(i))

        each(n, lambda i: c(i).start(), 1)
        each(n, lambda i: c(i).wait(), 1)

    def combine(buf, n, first_row, width, count):
        tops = [buf[j, :count, first_row : first_row + width] for j in range(n)]
        sums = [buf[j, :count, first_row + width : first_row + 2 * width] for j in range(n)]
        top = functools.reduce(jnp.maximum, tops)
        total = functools.reduce(jnp.add, [s * jnp.exp(m - top) for s, m in zip(sums, tops)])
        return top, total

    def pack(top, total):
        return jnp.concatenate([top, total, jnp.zeros((Z, 8 - 2 * nb, LANES), F32)], axis=1)

    stage(stat_voc, stat_voc_sem, voc, NV, lambda i: at(dx=i // 2, dc=mod(i, 2)))
    top_s, sum_s = combine(stat_voc, NV, 0, nb, Z)
    stat_y[y, :Z] = pack(top_s, sum_s)
    tops = [stat_voc[j, Z, 0:1] for j in range(NV)]
    sums = [stat_voc[j, Z, 1:2] for j in range(NV)]
    top_t = functools.reduce(jnp.maximum, tops)
    sum_t = functools.reduce(jnp.add, [s * jnp.exp(m - top_t) for s, m in zip(sums, tops)])
    used = lax.broadcasted_iota(jnp.int32, (1, LANES), 1) < R
    sum_t = jnp.where(used, sum_t, 1.0)
    stat_y[y, Z] = jnp.concatenate([top_t, jnp.log(sum_t), jnp.zeros((6, LANES), F32)], axis=0)

    stage(stat_y, stat_y_sem, y, Y, lambda i: at(dy=i))
    top_s, sum_s = combine(stat_y, Y, 0, nb, Z)
    stat_z[z, :Z] = pack(top_s, sum_s)
    for j in range(Y):
        stat_z[z, Z + j] = stat_y[j, Z]

    stage(stat_z, stat_z_sem, z, Z, lambda i: at(dz=i))
    top_s, sum_s = combine(stat_z, Z, 0, nb, Z)
    if q < LANES:
        sum_s = jnp.where(lax.broadcasted_iota(jnp.int32, sum_s.shape, 2) < q, sum_s, 1.0)
    stat_voc[0, :Z] = pack(top_s, jnp.log(sum_s))
    table_top = jnp.concatenate(
        [stat_z[i, Z + j, 0:1] for i in range(Z) for j in range(Y)], axis=0
    ).astype(BF16)
    table_log = jnp.concatenate(
        [stat_z[i, Z + j, 1:2] for i in range(Z) for j in range(Y)], axis=0
    )
    log_hi = table_log.astype(BF16)
    rest = table_log - log_hi.astype(F32)
    log_mid = rest.astype(BF16)
    log_lo = (rest - log_mid.astype(F32)).astype(BF16)

    ends = []
    total = jnp.int32(0)
    for j in range(lengths.shape[0]):
        total = total + lengths[j]
        ends.append(total - 1)

    own_block.wait()
    each(NT, lambda i: t_copy(i).wait(), 1)

    def mate(k):
        return copy(mate_send.at[k], mate_recv.at[k], mate_sem, k, at(dc=1))

    def r1a(k, i):
        return copy(
            folded.at[k, :, mod(x + i, X), :, pl.ds(0, QUARTER)],
            first_a.at[k, i - 1],
            r1a_sem,
            k * X + i,
            at(dx=i),
        )

    def r1b(k, i):
        return copy(
            folded.at[k, mod(y + i, Y), :, :, pl.ds(QUARTER, QUARTER)],
            first_b.at[k, i - 1],
            r1b_sem,
            k * Y + i,
            at(dy=i),
        )

    def gradient(k, acc):
        zc = mod(z + 1 + k, Z)
        here = pl.ds(pl.multiple_of(zc * CH, CH), CH)
        wanted = rows[here, :]
        block = wanted // R
        pick = (lax.broadcasted_iota(jnp.int32, (CH, NT), 1) == block).astype(F32).astype(BF16)
        lane = lax.broadcasted_iota(jnp.int32, (CH, LANES), 1) == (wanted - block * R)

        def take(table):
            return jnp.dot(pick, table, preferred_element_type=F32)

        def one(value):
            return jnp.sum(jnp.where(lane, value, 0.0), axis=1, keepdims=True)

        teacher_top = one(take(table_top))
        teacher_log = one(take(log_hi) + take(log_mid) + take(log_lo))
        stats = stat_voc[0, zc]

        def to_column(row):
            return jnp.sum(jnp.where(eye, row, 0.0), axis=1, keepdims=True)

        student_top = jnp.concatenate([to_column(stats[j : j + 1]) for j in range(nb)], axis=0)
        student_log = jnp.concatenate(
            [to_column(stats[nb + j : nb + j + 1]) for j in range(nb)], axis=0
        )
        place = lax.broadcasted_iota(jnp.int32, (CH, 1), 0) + zc * CH
        valid = jnp.ones((CH, 1), F32)
        for end in ends:
            valid = jnp.where(place == end, 0.0, valid)
        taken = jnp.dot(picks[here, :], teacher[...], preferred_element_type=F32) / TEMPERATURE
        log_teacher = (taken - teacher_top) - teacher_log
        log_student = (scores[here, :] - student_top) - student_log
        p_teacher = jnp.exp(log_teacher)
        p_student = jnp.exp(log_student)
        kl = jnp.sum(p_teacher * (log_teacher - log_student), axis=1, keepdims=True)
        grad = ((SCALE * TEMPERATURE) * valid * (p_student - p_teacher)).astype(BF16)
        slope[here, :] = grad

        def product(c):
            return lax.dot_general(
                grad,
                weights[pl.ds(pl.multiple_of(c * HALF, HALF), HALF), :],
                (((1,), (1,)), ((), ())),
                preferred_element_type=F32,
            )

        mate_send[k] = product(1 - core).astype(BF16)
        mate(k).start()
        own_half[mod(k, 2)] = product(core)
        return acc + jnp.sum(valid * kl, axis=0, keepdims=True)

    def fold_mate(k):
        mate(k).wait()
        value = own_half[mod(k, 2)] + mate_recv[k].astype(F32)
        folded[k] = value.astype(BF16).reshape(Y, X, 16, HALF)
        each(X, lambda i: r1a(k, i).start(), 1)
        each(Y, lambda i: r1b(k, i).start(), 1)

    acc = gradient(0, jnp.zeros((1, 1), F32))

    def forward(k, acc):
        acc = gradient(k, acc)
        fold_mate(k - 1)
        return acc

    acc = lax.fori_loop(1, Z, forward, acc)
    fold_mate(Z - 1)

    loss_voc[voc] = jnp.broadcast_to(acc, (8, LANES))
    stage(loss_voc, loss_voc_sem, voc, NV, lambda i: at(dx=i // 2, dc=mod(i, 2)))
    loss_y[y] = functools.reduce(jnp.add, [loss_voc[j] for j in range(NV)])
    stage(loss_y, loss_y_sem, y, Y, lambda i: at(dy=i))
    loss_z[z] = functools.reduce(jnp.add, [loss_y[j] for j in range(Y)])
    stage(loss_z, loss_z_sem, z, Z, lambda i: at(dz=i))
    loss = functools.reduce(jnp.add, [loss_z[j] for j in range(Z)])
    loss_out[...] = TEMPERATURE * TEMPERATURE * loss / (N - lengths.shape[0])

    def weight_part(b):
        wide = gathered[b // 2, mod(b, 2)].reshape(N, CS)
        value = lax.dot_general(
            wide, slope[...], (((0,), (0,)), ((), ())), preferred_element_type=F32
        )
        grad_weight[pl.ds(pl.multiple_of(b * CS, CS), CS), :] = value.astype(BF16)

    def r2a(k, i):
        return copy(
            second_a.at[k, mod(y + i, Y)], got_a.at[k, i - 1], r2a_sem, k * Y + i, at(dy=i)
        )

    def r2b(k, i):
        return copy(
            second_b.at[k, mod(x + i, X)], got_b.at[k, i - 1], r2b_sem, k * X + i, at(dx=i)
        )

    def fold_first(k):
        each(X, lambda i: r1a(k, i).wait(), 1)
        value = folded[k, :, x, :, :QUARTER].astype(F32)
        for i in range(X - 1):
            value = value + first_a[k, i].astype(F32)
        second_a[k] = value.astype(BF16)
        each(Y, lambda i: r2a(k, i).start(), 1)
        each(Y, lambda i: r1b(k, i).wait(), 1)
        value = folded[k, y, :, :, QUARTER:].astype(F32)
        for i in range(Y - 1):
            value = value + first_b[k, i].astype(F32)
        second_b[k] = value.astype(BF16)
        each(X, lambda i: r2b(k, i).start(), 1)

    def fold_second(k):
        each(Y, lambda i: r2a(k, i).wait(), 1)
        each(X, lambda i: r2b(k, i).wait(), 1)
        left = second_a[k, y].astype(F32)
        for i in range(Y - 1):
            left = left + got_a[k, i].astype(F32)
        right = second_b[k, x].astype(F32)
        for i in range(X - 1):
            right = right + got_b[k, i].astype(F32)
        last[0, k] = jnp.concatenate([left, right], axis=1).astype(BF16)

    def r3(k):
        return copy(last.at[0, k], last.at[1, k], r3_sem, k, at(dz=k + 1))

    weight_part(0)
    fold_first(0)

    def backward(k):
        weight_part(k)
        fold_first(k)
        fold_second(k - 1)
        r3(k - 1).start()

    each(Z, backward, 1)
    fold_second(Z - 1)
    each(Z - 1, lambda k: r3(k).wait())
    value = last[0, Z - 1].astype(F32)
    for k in range(Z - 1):
        value = value + last[1, k].astype(F32)
    final[...] = value
    swap = copy(final.at[pl.ds(pl.multiple_of((1 - core) * 8, 8), 8), :], final_recv, final_sem, 0, at(dc=1))
    swap.start()
    mine = jnp.where(core == 0, value[:8], value[8:])
    swap.wait()
    theirs = final_recv[...]
    grad_hidden[:, :HALF] = jnp.where(core == 0, mine, theirs).astype(BF16)
    grad_hidden[:, HALF:] = jnp.where(core == 0, theirs, mine).astype(BF16)


def body(dims, hidden, weights, mentor, rows, lengths):
    Z, Y, X, R, V, D = dims
    NT, NV, CH = Z * Y, X * 2, Y * R
    N, HALF, QUARTER, CS = Z * CH, D // 2, D // 4, D // NV
    vmem = pl.BlockSpec(memory_space=pltpu.VMEM)
    dma = lambda n: pltpu.SemaphoreType.DMA((2, n))
    loss, grad_hidden, grad_weight = pl.pallas_call(
        functools.partial(kernel, dims),
        out_shape=(
            jax.ShapeDtypeStruct((8, LANES), F32),
            jax.ShapeDtypeStruct((8, D), BF16),
            jax.ShapeDtypeStruct((D, V), BF16),
        ),
        in_specs=[vmem, vmem, vmem, vmem, pl.BlockSpec(memory_space=pltpu.SMEM)],
        out_specs=(vmem, vmem, vmem),
        scratch_shapes=[
            pltpu.VMEM((X, 2, Z, Y, R, CS), BF16),
            pltpu.VMEM((N, V), BF16),
            pltpu.VMEM((N, N), BF16),
            pltpu.VMEM((N, V), F32),
            pltpu.VMEM((N, V), BF16),
            pltpu.VMEM((Z, CH, HALF), BF16),
            pltpu.VMEM((Z, CH, HALF), BF16),
            pltpu.VMEM((2, CH, HALF), F32),
            pltpu.VMEM((Z, Y, X, 16, HALF), BF16),
            pltpu.VMEM((Z, X - 1, Y, 16, QUARTER), BF16),
            pltpu.VMEM((Z, Y - 1, X, 16, QUARTER), BF16),
            pltpu.VMEM((Z, Y, 16, QUARTER), BF16),
            pltpu.VMEM((Z, X, 16, QUARTER), BF16),
            pltpu.VMEM((Z, Y - 1, 16, QUARTER), BF16),
            pltpu.VMEM((Z, X - 1, 16, QUARTER), BF16),
            pltpu.VMEM((2, Z, 16, HALF), BF16),
            pltpu.VMEM((16, HALF), F32),
            pltpu.VMEM((8, HALF), F32),
            pltpu.VMEM((NV, Z + 1, 8, LANES), F32),
            pltpu.VMEM((Y, Z + 1, 8, LANES), F32),
            pltpu.VMEM((Z, Z + Y, 8, LANES), F32),
            pltpu.VMEM((NV, 8, LANES), F32),
            pltpu.VMEM((Y, 8, LANES), F32),
            pltpu.VMEM((Z, 8, LANES), F32),
            pltpu.SemaphoreType.DMA((2,)),
            dma(Z),
            dma(NT),
            dma(Y),
            dma(X),
            dma(X),
            dma(Y),
            dma(X),
            dma(Y),
            dma(NV),
            dma(Y),
            dma(Z),
            dma(NV),
            dma(Y),
            dma(Z),
            dma(Z),
            dma(Z * X),
            dma(Z * Y),
            dma(Z * Y),
            dma(Z * X),
            dma(Z),
            dma(1),
        ],
        compiler_params=pltpu.CompilerParams(
            collective_id=0, has_side_effects=True, vmem_limit_bytes=63 * 2**20
        ),
    )(hidden, weights, mentor, rows[:, None], lengths)
    return loss[0, 0], grad_hidden, grad_weight


def solution(mesh):
    NT, NV = mesh.shape["tok"], mesh.shape["voc"]
    Y = 1 << ((NT.bit_length() - 1) // 2)
    Z, X = NT // Y, NV // 2

    def run(hidden, weights, mentor, rows, lengths):
        N, D = hidden.shape
        dims = (Z, Y, X, N // NT, weights.shape[1] // (NT * NV), D)
        return jax.shard_map(
            functools.partial(body, dims),
            mesh=mesh,
            in_specs=(P("tok", None), P(None, ("voc", "tok")), P("tok", "voc"), P(), P()),
            out_specs=(P(), P(("tok", "voc"), None), P(None, ("voc", "tok"))),
            check_vma=False,
        )(hidden, weights, mentor, rows, lengths)

    return run
```

time: 1650 us -> 179 us (0.11)
  waiting for transfers between devices: 1330 us -> 0 us
  blocking collectives: 225 us -> 0 us
  Pallas kernels: 0 us -> 170 us
  matrix products: 37.1 us -> 0 us
    reduce_scatter x1 -> x0, waiting for transfers between devices: 1270 us -> none  [body(): lax.psum_scatter(lax.dot_general(derivative_routine, learner_projection_w...]
    pallas_call x0 -> x1, Pallas kernels: none -> 170 us  [body(): pl.pallas_call(functools.partial(kernel, dims), out_shape=(jax.ShapeDtype...]
    pmax x2 -> x0, blocking collectives: 151 us -> none  [body(): lax.pmax((local_student, local_teacher), ('tok', 'voc'))]
    psum x1 -> x0, blocking collectives: 73.2 us -> none  [body(): lax.psum((jnp.sum(exp_student, axis=1), jnp.sum(exp_teacher, axis=1), jnp...]
    all_to_all x1 -> x0, waiting for transfers between devices: 57.9 us -> none  [body(): lax.all_to_all(mentor_unscaled_scores, 'tok', split_axis=1, concat_axis=0...]
    dot_general x3 -> x0, matrix products: 37.1 us -> none  [the longest x1 14.1 us: body(): lax.dot_general(derivative_routine, learner_projection_weights, (((1,), (...]
  transfers between devices with their start and end apart: 3 -> 0, of which waited for: 2 -> 0; matrix products, arithmetic and copies ran while one was open for 2% -> 0% of each run, Pallas kernels for 0% -> 0%
where the time goes in v1:
time: 179 us
  Pallas kernels  170 us (95%)
  local copies, waits for them, and re-layouts  7.64 us (4%)
    pallas_call x1, Pallas kernels, body(): pl.pallas_call(functools.partial(kernel, dims), out_shape=(jax.ShapeDtype...  170 us
    unnamed x2, local copies, waits for them, and re-layouts  4.42 us

profile of v1, /device:TPU:1, one launch (start us, length us, event | category | flops | bytes accessed | tf_op | source)
XLA Modules:
  0.0 178.6 jit_solution(874664431921026090)
XLA Ops:
  0.6 2.0 %copy.8.rows = s32[2048,1]{1,0:T(8,128)} copy(s32[2048,1]{0,1:T(1,128)} %bitcast.2) | data formatting | bytes 16384 | tf_op jit(solution)/shard_map/broadcast_in_dim | solution.py:571
  2.7 170.3 %shard_map.76 = (f32[8,128]{1,0:T(8,128)}, bf16[8,2048]{1,0:T(8,128)(2,1)}, bf16[2048,512]{1,0:T(8,128)(2,1)}) custom-call(bf16[64,2048]{1,0:T(8,128)(2,1)} %hidden.1, bf16[2048,512]{1,0:T(8,128)(2,1)} %weights.1, bf16[64,16384]{1,0:T(8,128)(2,1)} %mentor.1, s32[2048,1]{1,0:T(8,128)} %copy.8.rows, s32[8]{0:T(128)} %lengths.1), custom_call_target="tpu_custom_call" | custom-call | tf_op jit(solution)/shard_map/pallas_call | solution.py:511
  173.0 1.2 slice.3
  174.2 1.4 copy.11
  175.6 3.0 %copy.12 = bf16[2048,512]{1,0:T(8,128)(2,1)} copy(bf16[2048,512]{1,0:T(8,128)(2,1)} %get-tuple-element.14) | data formatting | bytes 4194304

commit v2 on v1

--- a/solution.py
+++ b/solution.py
@@ -22,13 +22,16 @@
 def kernel(
     dims,
     hidden,
-    weights,
-    mentor,
+    weights_hbm,
+    mentor_hbm,
     rows,
     lengths,
     loss_out,
     grad_hidden,
     grad_weight,
+    weights,
+    mentor,
+    wanted_rows,
     gathered,
     teacher,
     picks,
@@ -50,6 +53,9 @@
     stat_voc,
     stat_y,
     stat_z,
+    mentor_voc,
+    mentor_y,
+    mentor_z,
     loss_voc,
     loss_y,
     loss_z,
@@ -60,11 +66,13 @@
     s2b_sem,
     s3a_sem,
     s3b_sem,
-    ca_sem,
-    cb_sem,
+    c_sem,
     stat_voc_sem,
     stat_y_sem,
     stat_z_sem,
+    mentor_voc_sem,
+    mentor_y_sem,
+    mentor_z_sem,
     loss_voc_sem,
     loss_y_sem,
     loss_z_sem,
@@ -89,6 +97,8 @@
     CP = CS // 2
     nb = max(1, CH // LANES)
     q = CH // nb
+    per_tile = 8 // nb
+    tiles = max(1, Z // per_tile)
 
     def at(dz=0, dy=0, dx=0, dc=0):
         return (
@@ -113,6 +123,11 @@
 
         lax.fori_loop(start, n, step, 0)
 
+    load_mentor = pltpu.make_async_copy(mentor_hbm, mentor, local_sem.at[2])
+    load_weights = pltpu.make_async_copy(weights_hbm, weights, local_sem.at[3])
+    load_mentor.start()
+    load_weights.start()
+
     barrier = pltpu.get_barrier_semaphore()
 
     def greet_tok(i):
@@ -145,7 +160,7 @@
     def t_copy(i):
         device = at(dz=i // Y, dy=mod(i, Y))
         return copy(
-            mentor.at[:, pl.ds(pl.multiple_of(device[0] * V, V), V)],
+            mentor_hbm.at[:, pl.ds(pl.multiple_of(device[0] * V, V), V)],
             teacher.at[pl.ds(pl.multiple_of(tok * R, R), R), :],
             t_sem,
             i,
@@ -154,12 +169,38 @@
 
     each(NT, lambda i: t_copy(i).start(), 1)
     own_block = pltpu.make_async_copy(
-        mentor.at[:, pl.ds(pl.multiple_of(tok * V, V), V)],
+        mentor_hbm.at[:, pl.ds(pl.multiple_of(tok * V, V), V)],
         teacher.at[pl.ds(pl.multiple_of(tok * R, R), R), :],
         local_sem.at[1],
     )
     own_block.start()
 
+    def stage(buf, sems, slot, n, target):
+        def c(i):
+            return copy(buf.at[slot], buf.at[slot], sems, i, target(i))
+
+        def start():
+            each(n, lambda i: c(i).start(), 1)
+
+        def wait():
+            each(n, lambda i: c(i).wait(), 1)
+
+        return start, wait
+
+    def three(voc_buf, y_buf, z_buf, voc_sem, y_sem, z_sem):
+        return (
+            stage(voc_buf, voc_sem, voc, NV, lambda i: at(dx=i // 2, dc=mod(i, 2))),
+            stage(y_buf, y_sem, y, Y, lambda i: at(dy=i)),
+            stage(z_buf, z_sem, z, Z, lambda i: at(dz=i)),
+        )
+
+    stat_stages = three(stat_voc, stat_y, stat_z, stat_voc_sem, stat_y_sem, stat_z_sem)
+    mentor_stages = three(
+        mentor_voc, mentor_y, mentor_z, mentor_voc_sem, mentor_y_sem, mentor_z_sem
+    )
+    loss_stages = three(loss_voc, loss_y, loss_z, loss_voc_sem, loss_y_sem, loss_z_sem)
+
+    load_mentor.wait()
     eye = lax.broadcasted_iota(jnp.int32, (q, LANES), 0) == lax.broadcasted_iota(
         jnp.int32, (q, LANES), 1
     )
@@ -194,68 +235,63 @@
     def to_lanes(column, mask):
         return jnp.sum(jnp.where(mask, column, 0.0), axis=0, keepdims=True)
 
-    stat_voc[voc, Z] = jnp.concatenate(
+    mentor_voc[voc] = jnp.concatenate(
         [to_lanes(top_t, eye_rows), to_lanes(sum_t, eye_rows), jnp.zeros((6, LANES), F32)], axis=0
     )
+    mentor_stages[0][0]()
+
+    def to_column(row):
+        return jnp.sum(jnp.where(eye[:, : row.shape[1]], row, 0.0), axis=1, keepdims=True)
 
     def fill_picks(k):
         here = pl.ds(pl.multiple_of(k * CH, CH), CH)
-        wanted = rows[here, :]
+        parts = [to_column(rows[pl.ds(k * nb + j, 1), :].astype(F32)) for j in range(nb)]
+        wanted = jnp.concatenate(parts, axis=0).astype(jnp.int32)
+        wanted_rows[here, :] = wanted
         places = lax.broadcasted_iota(jnp.int32, (CH, N), 1)
         picks[here, :] = jnp.where(places == wanted, 1.0, 0.0).astype(BF16)
 
     each(Z, fill_picks)
 
-    own_columns.wait()
-    each(Z, lambda i: s1(i).wait(), 1)
+    mentor_stages[0][1]()
+    tops = [mentor_voc[j, 0:1] for j in range(NV)]
+    sums = [mentor_voc[j, 1:2] for j in range(NV)]
+    top_t = functools.reduce(jnp.maximum, tops)
+    sum_t = functools.reduce(jnp.add, [s * jnp.exp(m - top_t) for s, m in zip(sums, tops)])
+    used = lax.broadcasted_iota(jnp.int32, (1, LANES), 1) < R
+    sum_t = jnp.where(used, sum_t, 1.0)
+    mentor_y[y] = jnp.concatenate([top_t, jnp.log(sum_t), jnp.zeros((6, LANES), F32)], axis=0)
+    mentor_stages[1][0]()
+
     first, second = pl.ds(0, CP), pl.ds(CP, CP)
-
-    def s2a(i):
-        block = gathered.at[x, core, :, y, :, first]
-        return copy(block, block, s2a_sem, i, at(dy=i))
-
-    def s2b(i):
-        block = gathered.at[x, core, :, y, :, second]
-        return copy(block, block, s2b_sem, i, at(dx=i))
-
-    each(Y, lambda i: s2a(i).start(), 1)
-    each(X, lambda i: s2b(i).start(), 1)
-
-    def s3a(i):
-        block = gathered.at[x, core, :, :, :, first]
-        return copy(block, block, s3a_sem, i, at(dx=i))
-
-    def s3b(i):
-        block = gathered.at[:, core, :, y, :, second]
-        return copy(block, block, s3b_sem, i, at(dy=i))
-
-    def ca(i):
-        block = gathered.at[mod(x + X - i, X), core, :, :, :, first]
-        return copy(block, block, ca_sem, i, at(dc=1))
-
-    def cb(i):
-        block = gathered.at[:, core, :, mod(y + Y - i, Y), :, second]
-        return copy(block, block, cb_sem, i, at(dc=1))
-
-    each(Y, lambda i: s2a(i).wait(), 1)
-    each(X, lambda i: s3a(i).start(), 1)
-    each(X, lambda i: s2b(i).wait(), 1)
-    each(Y, lambda i: s3b(i).start(), 1)
-    ca(0).start()
-    cb(0).start()
-
-    def on_x(i):
-        s3a(i).wait()
-        ca(i).start()
-
-    def on_y(i):
-        s3b(i).wait()
-        cb(i).start()
-
-    each(X, on_x, 1)
-    each(Y, on_y, 1)
-    each(X, lambda i: ca(i).wait())
-    each(Y, lambda i: cb(i).wait())
+    load_weights.wait()
+    stat_voc[voc] = jnp.zeros((2 * tiles, 8, LANES), F32)
+
+    def away(j):
+        return mod(jnp.where(mod(j, 2) == 1, (j + 1) // 2, Z - j // 2), Z)
+
+    def chunk(j):
+        return mod(z + Z - away(j), Z)
+
+    def s2a(j, i):
+        block = gathered.at[x, core, chunk(j), y, :, first]
+        return copy(block, block, s2a_sem, j * Y + i, at(dy=i))
+
+    def s2b(j, i):
+        block = gathered.at[x, core, chunk(j), y, :, second]
+        return copy(block, block, s2b_sem, j * X + i, at(dx=i))
+
+    def s3a(j, i):
+        block = gathered.at[x, core, chunk(j), :, :, first]
+        return copy(block, block, s3a_sem, j * X + i, at(dx=i))
+
+    def s3b(j, i):
+        block = gathered.at[:, core, chunk(j), y, :, second]
+        return copy(block, block, s3b_sem, j * Y + i, at(dy=i))
+
+    def c(j):
+        block = gathered.at[:, core, chunk(j)]
+        return copy(block, block, c_sem, j, at(dc=1))
 
     def hidden_of(b, k):
         return gathered[b // 2, b % 2, k].reshape(CH, CS)
@@ -267,63 +303,87 @@
         scores[here, :] = value
         top = jnp.max(value, axis=1, keepdims=True)
         total = jnp.sum(jnp.exp(value - top), axis=1, keepdims=True)
-        parts = [to_lanes(top[j * q : (j + 1) * q], eye) for j in range(nb)]
-        parts += [to_lanes(total[j * q : (j + 1) * q], eye) for j in range(nb)]
-        parts.append(jnp.zeros((8 - 2 * nb, LANES), F32))
-        stat_voc[voc, k] = jnp.concatenate(parts, axis=0)
-
-    each(Z, score)
-
-    def stage(buf, sems, slot, n, target, count=None):
-        def c(i):
-            block = buf.at[slot] if count is None else buf.at[slot, pl.ds(0, count)]
-            return copy(block, block, sems, i, target(i))
-
-        each(n, lambda i: c(i).start(), 1)
-        each(n, lambda i: c(i).wait(), 1)
-
-    def combine(buf, n, first_row, width, count):
-        tops = [buf[j, :count, first_row : first_row + width] for j in range(n)]
-        sums = [buf[j, :count, first_row + width : first_row + 2 * width] for j in range(n)]
+        group = lax.broadcasted_iota(jnp.int32, (8, LANES), 0) // nb == mod(k, per_tile)
+
+        def put(column, tile):
+            parts = [to_lanes(column[j * q : (j + 1) * q], eye) for j in range(nb)]
+            value = jnp.concatenate(parts * per_tile, axis=0)
+            stat_voc[voc, tile] = jnp.where(group, value, stat_voc[voc, tile])
+
+        put(top, k // per_tile)
+        put(total, tiles + k // per_tile)
+
+    def gather(j):
+        @pl.when(j == 0)
+        def _():
+            own_columns.wait()
+
+        @pl.when((j > 0) & (j < Z))
+        def _():
+            s1(away(j)).wait()
+
+        @pl.when(j < Z)
+        def _():
+            each(Y, lambda i: s2a(j, i).start(), 1)
+            each(X, lambda i: s2b(j, i).start(), 1)
+
+        @pl.when((j >= 1) & (j < Z + 1))
+        def _():
+            each(Y, lambda i: s2a(j - 1, i).wait(), 1)
+            each(X, lambda i: s3a(j - 1, i).start(), 1)
+            each(X, lambda i: s2b(j - 1, i).wait(), 1)
+            each(Y, lambda i: s3b(j - 1, i).start(), 1)
+
+        @pl.when((j >= 2) & (j < Z + 2))
+        def _():
+            each(X, lambda i: s3a(j - 2, i).wait(), 1)
+            each(Y, lambda i: s3b(j - 2, i).wait(), 1)
+            c(j - 2).start()
+
+        @pl.when(j >= 3)
+        def _():
+            c(j - 3).wait()
+            score(chunk(j - 3))
+
+    each(Z + 3, gather)
+
+    def combine(buf, n):
+        tops = [buf[j, :tiles] for j in range(n)]
+        sums = [buf[j, tiles:] for j in range(n)]
         top = functools.reduce(jnp.maximum, tops)
         total = functools.reduce(jnp.add, [s * jnp.exp(m - top) for s, m in zip(sums, tops)])
         return top, total
 
-    def pack(top, total):
-        return jnp.concatenate([top, total, jnp.zeros((Z, 8 - 2 * nb, LANES), F32)], axis=1)
-
-    stage(stat_voc, stat_voc_sem, voc, NV, lambda i: at(dx=i // 2, dc=mod(i, 2)))
-    top_s, sum_s = combine(stat_voc, NV, 0, nb, Z)
-    stat_y[y, :Z] = pack(top_s, sum_s)
-    tops = [stat_voc[j, Z, 0:1] for j in range(NV)]
-    sums = [stat_voc[j, Z, 1:2] for j in range(NV)]
-    top_t = functools.reduce(jnp.maximum, tops)
-    sum_t = functools.reduce(jnp.add, [s * jnp.exp(m - top_t) for s, m in zip(sums, tops)])
-    used = lax.broadcasted_iota(jnp.int32, (1, LANES), 1) < R
-    sum_t = jnp.where(used, sum_t, 1.0)
-    stat_y[y, Z] = jnp.concatenate([top_t, jnp.log(sum_t), jnp.zeros((6, LANES), F32)], axis=0)
-
-    stage(stat_y, stat_y_sem, y, Y, lambda i: at(dy=i))
-    top_s, sum_s = combine(stat_y, Y, 0, nb, Z)
-    stat_z[z, :Z] = pack(top_s, sum_s)
+    stat_stages[0][0]()
+    mentor_stages[1][1]()
     for j in range(Y):
-        stat_z[z, Z + j] = stat_y[j, Z]
-
-    stage(stat_z, stat_z_sem, z, Z, lambda i: at(dz=i))
-    top_s, sum_s = combine(stat_z, Z, 0, nb, Z)
-    if q < LANES:
-        sum_s = jnp.where(lax.broadcasted_iota(jnp.int32, sum_s.shape, 2) < q, sum_s, 1.0)
-    stat_voc[0, :Z] = pack(top_s, jnp.log(sum_s))
+        mentor_z[z, j] = mentor_y[j]
+    mentor_stages[2][0]()
+    stat_stages[0][1]()
+    top_s, sum_s = combine(stat_voc, NV)
+    stat_y[y, :tiles] = top_s
+    stat_y[y, tiles:] = sum_s
+    stat_stages[1][0]()
+    stat_stages[1][1]()
+    top_s, sum_s = combine(stat_y, Y)
+    stat_z[z, :tiles] = top_s
+    stat_z[z, tiles:] = sum_s
+    stat_stages[2][0]()
+    mentor_stages[2][1]()
     table_top = jnp.concatenate(
-        [stat_z[i, Z + j, 0:1] for i in range(Z) for j in range(Y)], axis=0
+        [mentor_z[i, j, 0:1] for i in range(Z) for j in range(Y)], axis=0
     ).astype(BF16)
     table_log = jnp.concatenate(
-        [stat_z[i, Z + j, 1:2] for i in range(Z) for j in range(Y)], axis=0
+        [mentor_z[i, j, 1:2] for i in range(Z) for j in range(Y)], axis=0
     )
     log_hi = table_log.astype(BF16)
     rest = table_log - log_hi.astype(F32)
     log_mid = rest.astype(BF16)
     log_lo = (rest - log_mid.astype(F32)).astype(BF16)
+    stat_stages[2][1]()
+    top_s, sum_s = combine(stat_z, Z)
+    stat_voc[0, :tiles] = top_s
+    stat_voc[0, tiles:] = jnp.log(jnp.where(sum_s > 0.0, sum_s, 1.0))
 
     ends = []
     total = jnp.int32(0)
@@ -355,10 +415,12 @@
             at(dy=i),
         )
 
-    def gradient(k, acc):
+    loss_voc[voc] = jnp.zeros((8, LANES), F32)
+
+    def gradient(k):
         zc = mod(z + 1 + k, Z)
         here = pl.ds(pl.multiple_of(zc * CH, CH), CH)
-        wanted = rows[here, :]
+        wanted = wanted_rows[here, :]
         block = wanted // R
         pick = (lax.broadcasted_iota(jnp.int32, (CH, NT), 1) == block).astype(F32).astype(BF16)
         lane = lax.broadcasted_iota(jnp.int32, (CH, LANES), 1) == (wanted - block * R)
@@ -371,15 +433,19 @@
 
         teacher_top = one(take(table_top))
         teacher_log = one(take(log_hi) + take(log_mid) + take(log_lo))
-        stats = stat_voc[0, zc]
-
-        def to_column(row):
-            return jnp.sum(jnp.where(eye, row, 0.0), axis=1, keepdims=True)
-
-        student_top = jnp.concatenate([to_column(stats[j : j + 1]) for j in range(nb)], axis=0)
-        student_log = jnp.concatenate(
-            [to_column(stats[nb + j : nb + j + 1]) for j in range(nb)], axis=0
-        )
+        row_of = lax.broadcasted_iota(jnp.int32, (8, LANES), 0)
+
+        def student(tile):
+            value = stat_voc[0, tile + zc // per_tile]
+            first_row = mod(zc, per_tile) * nb
+            picked = [
+                jnp.sum(jnp.where(row_of == first_row + j, value, 0.0), axis=0, keepdims=True)
+                for j in range(nb)
+            ]
+            return jnp.concatenate([to_column(row) for row in picked], axis=0)
+
+        student_top = student(0)
+        student_log = student(tiles)
         place = lax.broadcasted_iota(jnp.int32, (CH, 1), 0) + zc * CH
         valid = jnp.ones((CH, 1), F32)
         for end in ends:
@@ -404,7 +470,7 @@
         mate_send[k] = product(1 - core).astype(BF16)
         mate(k).start()
         own_half[mod(k, 2)] = product(core)
-        return acc + jnp.sum(valid * kl, axis=0, keepdims=True)
+        loss_voc[voc] = loss_voc[voc] + jnp.sum(valid * kl, axis=0, keepdims=True)
 
     def fold_mate(k):
         mate(k).wait()
@@ -412,25 +478,6 @@
         folded[k] = value.astype(BF16).reshape(Y, X, 16, HALF)
         each(X, lambda i: r1a(k, i).start(), 1)
         each(Y, lambda i: r1b(k, i).start(), 1)
-
-    acc = gradient(0, jnp.zeros((1, 1), F32))
-
-    def forward(k, acc):
-        acc = gradient(k, acc)
-        fold_mate(k - 1)
-        return acc
-
-    acc = lax.fori_loop(1, Z, forward, acc)
-    fold_mate(Z - 1)
-
-    loss_voc[voc] = jnp.broadcast_to(acc, (8, LANES))
-    stage(loss_voc, loss_voc_sem, voc, NV, lambda i: at(dx=i // 2, dc=mod(i, 2)))
-    loss_y[y] = functools.reduce(jnp.add, [loss_voc[j] for j in range(NV)])
-    stage(loss_y, loss_y_sem, y, Y, lambda i: at(dy=i))
-    loss_z[z] = functools.reduce(jnp.add, [loss_y[j] for j in range(Y)])
-    stage(loss_z, loss_z_sem, z, Z, lambda i: at(dz=i))
-    loss = functools.reduce(jnp.add, [loss_z[j] for j in range(Z)])
-    loss_out[...] = TEMPERATURE * TEMPERATURE * loss / (N - lengths.shape[0])
 
     def weight_part(b):
         wide = gathered[b // 2, mod(b, 2)].reshape(N, CS)
@@ -477,17 +524,54 @@
     def r3(k):
         return copy(last.at[0, k], last.at[1, k], r3_sem, k, at(dz=k + 1))
 
-    weight_part(0)
-    fold_first(0)
-
-    def backward(k):
-        weight_part(k)
-        fold_first(k)
-        fold_second(k - 1)
-        r3(k - 1).start()
-
-    each(Z, backward, 1)
-    fold_second(Z - 1)
+    LAG1, LAG2 = 3, 5
+
+    def turn(j):
+        @pl.when(j < Z)
+        def _():
+            gradient(j)
+
+        @pl.when((j >= 1) & (j < Z + 1))
+        def _():
+            fold_mate(j - 1)
+
+        @pl.when((j >= LAG1) & (j < Z + LAG1))
+        def _():
+            fold_first(j - LAG1)
+
+        @pl.when((j >= LAG2) & (j < Z + LAG2))
+        def _():
+            fold_second(j - LAG2)
+
+        @pl.when((j >= LAG2) & (j < Z + LAG2 - 1))
+        def _():
+            r3(j - LAG2).start()
+
+        @pl.when(j == Z)
+        def _():
+            loss_stages[0][0]()
+
+        @pl.when(j == Z + 1)
+        def _():
+            loss_stages[0][1]()
+            loss_y[y] = functools.reduce(jnp.add, [loss_voc[i] for i in range(NV)])
+            loss_stages[1][0]()
+
+        @pl.when(j == Z + 2)
+        def _():
+            loss_stages[1][1]()
+            loss_z[z] = functools.reduce(jnp.add, [loss_y[i] for i in range(Y)])
+            loss_stages[2][0]()
+
+        @pl.when((j >= Z) & (j < Z + NV // 2))
+        def _():
+            weight_part(2 * (j - Z))
+            weight_part(2 * (j - Z) + 1)
+
+    each(Z + LAG2, turn)
+    loss_stages[2][1]()
+    loss = functools.reduce(jnp.add, [loss_z[j] for j in range(Z)])
+    loss_out[...] = TEMPERATURE * TEMPERATURE * loss / (N - lengths.shape[0])
     each(Z - 1, lambda k: r3(k).wait())
     value = last[0, Z - 1].astype(F32)
     for k in range(Z - 1):
@@ -507,6 +591,9 @@
     NT, NV, CH = Z * Y, X * 2, Y * R
     N, HALF, QUARTER, CS = Z * CH, D // 2, D // 4, D // NV
     vmem = pl.BlockSpec(memory_space=pltpu.VMEM)
+    anywhere = pl.BlockSpec(memory_space=pl.ANY)
+    nb = max(1, CH // LANES)
+    tiles = max(1, Z * nb // 8)
     dma = lambda n: pltpu.SemaphoreType.DMA((2, n))
     loss, grad_hidden, grad_weight = pl.pallas_call(
         functools.partial(kernel, dims),
@@ -515,9 +602,12 @@
             jax.ShapeDtypeStruct((8, D), BF16),
             jax.ShapeDtypeStruct((D, V), BF16),
         ),
-        in_specs=[vmem, vmem, vmem, vmem, pl.BlockSpec(memory_space=pltpu.SMEM)],
+        in_specs=[anywhere, anywhere, anywhere, vmem, pl.BlockSpec(memory_space=pltpu.SMEM)],
         out_specs=(vmem, vmem, vmem),
         scratch_shapes=[
+            pltpu.VMEM((D, V), BF16),
+            pltpu.VMEM((R, V * NT), BF16),
+            pltpu.VMEM((N, 1), jnp.int32),
             pltpu.VMEM((X, 2, Z, Y, R, CS), BF16),
             pltpu.VMEM((N, V), BF16),
             pltpu.VMEM((N, N), BF16),
@@ -536,21 +626,26 @@
             pltpu.VMEM((2, Z, 16, HALF), BF16),
             pltpu.VMEM((16, HALF), F32),
             pltpu.VMEM((8, HALF), F32),
-            pltpu.VMEM((NV, Z + 1, 8, LANES), F32),
-            pltpu.VMEM((Y, Z + 1, 8, LANES), F32),
-            pltpu.VMEM((Z, Z + Y, 8, LANES), F32),
+            pltpu.VMEM((NV, 2 * tiles, 8, LANES), F32),
+            pltpu.VMEM((Y, 2 * tiles, 8, LANES), F32),
+            pltpu.VMEM((Z, 2 * tiles, 8, LANES), F32),
+            pltpu.VMEM((NV, 8, LANES), F32),
+            pltpu.VMEM((Y, 8, LANES), F32),
+            pltpu.VMEM((Z, Y, 8, LANES), F32),
             pltpu.VMEM((NV, 8, LANES), F32),
             pltpu.VMEM((Y, 8, LANES), F32),
             pltpu.VMEM((Z, 8, LANES), F32),
-            pltpu.SemaphoreType.DMA((2,)),
+            pltpu.SemaphoreType.DMA((4,)),
             dma(Z),
             dma(NT),
+            dma(Z * Y),
+            dma(Z * X),
+            dma(Z * X),
+            dma(Z * Y),
+            dma(Z),
+            dma(NV),
             dma(Y),
-            dma(X),
-            dma(X),
-            dma(Y),
-            dma(X),
-            dma(Y),
+            dma(Z),
             dma(NV),
             dma(Y),
             dma(Z),
@@ -568,7 +663,7 @@
         compiler_params=pltpu.CompilerParams(
             collective_id=0, has_side_effects=True, vmem_limit_bytes=63 * 2**20
         ),
-    )(hidden, weights, mentor, rows[:, None], lengths)
+    )(hidden, weights, mentor, rows.reshape(Z * nb, CH // nb), lengths)
     return loss[0, 0], grad_hidden, grad_weight
 
 

time: 179 us -> 146 us (0.82)
  Pallas kernels: 170 us -> 139 us
  local copies, waits for them, and re-layouts: 7.64 us -> 5.6 us
    pallas_call x1, Pallas kernels: 170 us -> 139 us  [body(): pl.pallas_call(functools.partial(kernel, dims), out_shape=(jax.ShapeDtype...]
    broadcast_in_dim x1 -> x0, local copies, waits for them, and re-layouts: 2.04 us -> none  [body(): rows[:, None]]
where the time goes in v2:
time: 146 us
  Pallas kernels  139 us (95%)
  local copies, waits for them, and re-layouts  5.6 us (4%)
    pallas_call x1, Pallas kernels, body(): pl.pallas_call(functools.partial(kernel, dims), out_shape=(jax.ShapeDtype...  139 us
    unnamed x2, local copies, waits for them, and re-layouts  4.42 us

profile of v2, /device:TPU:1, one launch (start us, length us, event | category | flops | bytes accessed | tf_op | source)
XLA Modules:
  0.0 145.5 jit_solution(11088173864134884439)
XLA Ops:
  0.6 139.3 %shard_map.76 = (f32[8,128]{1,0:T(8,128)}, bf16[8,2048]{1,0:T(8,128)(2,1)}, bf16[2048,512]{1,0:T(8,128)(2,1)}) custom-call(bf16[64,2048]{1,0:T(8,128)(2,1)} %hidden.1, bf16[2048,512]{1,0:T(8,128)(2,1)} %weights_hbm.1, bf16[64,16384]{1,0:T(8,128)(2,1)} %mentor_hbm.1, s32[16,128]{1,0:T(8,128)} %bitcast.2, s32[8]{0:T(128)} %lengths.1), custom_call_target="tpu_custom_call" | custom-call | tf_op jit(solution)/shard_map/pallas_call | solution.py:598
  139.9 1.2 slice.3
  141.1 1.4 copy.10
  142.5 3.0 %copy.11 = bf16[2048,512]{1,0:T(8,128)(2,1)} copy(bf16[2048,512]{1,0:T(8,128)(2,1)} %get-tuple-element.14) | data formatting | bytes 4194304

commit v3 on v2

--- a/solution.py
+++ b/solution.py
@@ -32,6 +32,8 @@
     weights,
     mentor,
     wanted_rows,
+    run_top,
+    run_sum,
     gathered,
     teacher,
     picks,
@@ -47,6 +49,11 @@
     second_b,
     got_a,
     got_b,
+    first_c,
+    second_c,
+    got_c,
+    third_c,
+    got_d,
     last,
     final,
     final_recv,
@@ -81,6 +88,9 @@
     r1b_sem,
     r2a_sem,
     r2b_sem,
+    r1c_sem,
+    r2c_sem,
+    r3c_sem,
     r3_sem,
     final_sem,
 ):
@@ -92,7 +102,8 @@
     CH = Y * R
     N = Z * CH
     HALF = D // 2
-    QUARTER = D // 4
+    PC = HALF // 4
+    PA = (HALF - PC) // 2
     CS = D // NV
     CP = CS // 2
     nb = max(1, CH // LANES)
@@ -116,6 +127,9 @@
             device_id_type=MESH,
         )
 
+    def join(block, sems, index=0):
+        copy(block, block, sems, index, at(dc=1)).wait()
+
     def each(n, body, start=0):
         def step(i, carry):
             body(i)
@@ -163,7 +177,7 @@
             mentor_hbm.at[:, pl.ds(pl.multiple_of(device[0] * V, V), V)],
             teacher.at[pl.ds(pl.multiple_of(tok * R, R), R), :],
             t_sem,
-            i,
+            0,
             device,
         )
 
@@ -177,13 +191,13 @@
 
     def stage(buf, sems, slot, n, target):
         def c(i):
-            return copy(buf.at[slot], buf.at[slot], sems, i, target(i))
+            return copy(buf.at[slot], buf.at[slot], sems, 0, target(i))
 
         def start():
             each(n, lambda i: c(i).start(), 1)
 
         def wait():
-            each(n, lambda i: c(i).wait(), 1)
+            join(buf.at[pl.ds(0, n - 1)], sems)
 
         return start, wait
 
@@ -200,7 +214,6 @@
     )
     loss_stages = three(loss_voc, loss_y, loss_z, loss_voc_sem, loss_y_sem, loss_z_sem)
 
-    load_mentor.wait()
     eye = lax.broadcasted_iota(jnp.int32, (q, LANES), 0) == lax.broadcasted_iota(
         jnp.int32, (q, LANES), 1
     )
@@ -217,28 +230,34 @@
             total = op(total, value[:, j * LANES : (j + 1) * LANES])
         return total
 
-    top_t = lax.fori_loop(
-        0,
-        NT,
-        lambda i, m: jnp.maximum(m, fold(jnp.maximum, columns_of(i))),
-        jnp.full((R, LANES), -jnp.inf, F32),
-    )
-    top_t = jnp.max(top_t, axis=1, keepdims=True)
-    sum_t = lax.fori_loop(
-        0,
-        NT,
-        lambda i, s: s + fold(jnp.add, jnp.exp(columns_of(i) - top_t)),
-        jnp.zeros((R, LANES), F32),
-    )
-    sum_t = jnp.sum(sum_t, axis=1, keepdims=True)
-
     def to_lanes(column, mask):
         return jnp.sum(jnp.where(mask, column, 0.0), axis=0, keepdims=True)
 
-    mentor_voc[voc] = jnp.concatenate(
-        [to_lanes(top_t, eye_rows), to_lanes(sum_t, eye_rows), jnp.zeros((6, LANES), F32)], axis=0
-    )
-    mentor_stages[0][0]()
+    run_top[...] = jnp.full((R, LANES), -jnp.inf, F32)
+    run_sum[...] = jnp.zeros((R, LANES), F32)
+
+    def mentor_part(j):
+        old = run_top[...]
+        top = lax.fori_loop(
+            j * Y, (j + 1) * Y, lambda i, m: jnp.maximum(m, fold(jnp.maximum, columns_of(i))), old
+        )
+        wide = jnp.concatenate([top] * (V // LANES), axis=1)
+        run_sum[...] = lax.fori_loop(
+            j * Y,
+            (j + 1) * Y,
+            lambda i, s: s + fold(jnp.add, jnp.exp(columns_of(i) - wide)),
+            run_sum[...] * jnp.exp(old - top),
+        )
+        run_top[...] = top
+
+    def mentor_done():
+        top_t = jnp.max(run_top[...], axis=1, keepdims=True)
+        sum_t = jnp.sum(run_sum[...] * jnp.exp(run_top[...] - top_t), axis=1, keepdims=True)
+        mentor_voc[voc] = jnp.concatenate(
+            [to_lanes(top_t, eye_rows), to_lanes(sum_t, eye_rows), jnp.zeros((6, LANES), F32)],
+            axis=0,
+        )
+        mentor_stages[0][0]()
 
     def to_column(row):
         return jnp.sum(jnp.where(eye[:, : row.shape[1]], row, 0.0), axis=1, keepdims=True)
@@ -251,20 +270,24 @@
         places = lax.broadcasted_iota(jnp.int32, (CH, N), 1)
         picks[here, :] = jnp.where(places == wanted, 1.0, 0.0).astype(BF16)
 
-    each(Z, fill_picks)
-
-    mentor_stages[0][1]()
-    tops = [mentor_voc[j, 0:1] for j in range(NV)]
-    sums = [mentor_voc[j, 1:2] for j in range(NV)]
-    top_t = functools.reduce(jnp.maximum, tops)
-    sum_t = functools.reduce(jnp.add, [s * jnp.exp(m - top_t) for s, m in zip(sums, tops)])
-    used = lax.broadcasted_iota(jnp.int32, (1, LANES), 1) < R
-    sum_t = jnp.where(used, sum_t, 1.0)
-    mentor_y[y] = jnp.concatenate([top_t, jnp.log(sum_t), jnp.zeros((6, LANES), F32)], axis=0)
-    mentor_stages[1][0]()
+    def mentor_second():
+        mentor_stages[0][1]()
+        tops = [mentor_voc[j, 0:1] for j in range(NV)]
+        sums = [mentor_voc[j, 1:2] for j in range(NV)]
+        top_t = functools.reduce(jnp.maximum, tops)
+        sum_t = functools.reduce(jnp.add, [s * jnp.exp(m - top_t) for s, m in zip(sums, tops)])
+        used = lax.broadcasted_iota(jnp.int32, (1, LANES), 1) < R
+        sum_t = jnp.where(used, sum_t, 1.0)
+        mentor_y[y] = jnp.concatenate([top_t, jnp.log(sum_t), jnp.zeros((6, LANES), F32)], axis=0)
+        mentor_stages[1][0]()
+
+    def mentor_third():
+        mentor_stages[1][1]()
+        for j in range(Y):
+            mentor_z[z, j] = mentor_y[j]
+        mentor_stages[2][0]()
 
     first, second = pl.ds(0, CP), pl.ds(CP, CP)
-    load_weights.wait()
     stat_voc[voc] = jnp.zeros((2 * tiles, 8, LANES), F32)
 
     def away(j):
@@ -275,19 +298,19 @@
 
     def s2a(j, i):
         block = gathered.at[x, core, chunk(j), y, :, first]
-        return copy(block, block, s2a_sem, j * Y + i, at(dy=i))
+        return copy(block, block, s2a_sem, j, at(dy=i))
 
     def s2b(j, i):
         block = gathered.at[x, core, chunk(j), y, :, second]
-        return copy(block, block, s2b_sem, j * X + i, at(dx=i))
+        return copy(block, block, s2b_sem, j, at(dx=i))
 
     def s3a(j, i):
         block = gathered.at[x, core, chunk(j), :, :, first]
-        return copy(block, block, s3a_sem, j * X + i, at(dx=i))
+        return copy(block, block, s3a_sem, j, at(dx=i))
 
     def s3b(j, i):
         block = gathered.at[:, core, chunk(j), y, :, second]
-        return copy(block, block, s3b_sem, j * Y + i, at(dy=i))
+        return copy(block, block, s3b_sem, j, at(dy=i))
 
     def c(j):
         block = gathered.at[:, core, chunk(j)]
@@ -317,6 +340,7 @@
         @pl.when(j == 0)
         def _():
             own_columns.wait()
+            load_mentor.wait()
 
         @pl.when((j > 0) & (j < Z))
         def _():
@@ -329,16 +353,37 @@
 
         @pl.when((j >= 1) & (j < Z + 1))
         def _():
-            each(Y, lambda i: s2a(j - 1, i).wait(), 1)
+            join(gathered.at[x, core, chunk(j - 1), pl.ds(0, Y - 1), :, first], s2a_sem, j - 1)
             each(X, lambda i: s3a(j - 1, i).start(), 1)
-            each(X, lambda i: s2b(j - 1, i).wait(), 1)
+            join(gathered.at[pl.ds(0, X - 1), core, chunk(j - 1), y, :, second], s2b_sem, j - 1)
             each(Y, lambda i: s3b(j - 1, i).start(), 1)
 
         @pl.when((j >= 2) & (j < Z + 2))
         def _():
-            each(X, lambda i: s3a(j - 2, i).wait(), 1)
-            each(Y, lambda i: s3b(j - 2, i).wait(), 1)
+            join(gathered.at[pl.ds(0, X - 1), core, chunk(j - 2), :, :, first], s3a_sem, j - 2)
+            join(gathered.at[:, core, chunk(j - 2), pl.ds(0, Y - 1), :, second], s3b_sem, j - 2)
             c(j - 2).start()
+
+        @pl.when(j < Z)
+        def _():
+            mentor_part(j)
+            fill_picks(j)
+
+        @pl.when(j == Z - 1)
+        def _():
+            mentor_done()
+
+        @pl.when(j == Z)
+        def _():
+            mentor_second()
+
+        @pl.when(j == Z + 1)
+        def _():
+            mentor_third()
+
+        @pl.when(j == 3)
+        def _():
+            load_weights.wait()
 
         @pl.when(j >= 3)
         def _():
@@ -355,10 +400,6 @@
         return top, total
 
     stat_stages[0][0]()
-    mentor_stages[1][1]()
-    for j in range(Y):
-        mentor_z[z, j] = mentor_y[j]
-    mentor_stages[2][0]()
     stat_stages[0][1]()
     top_s, sum_s = combine(stat_voc, NV)
     stat_y[y, :tiles] = top_s
@@ -392,27 +433,32 @@
         ends.append(total - 1)
 
     own_block.wait()
-    each(NT, lambda i: t_copy(i).wait(), 1)
+    join(teacher.at[pl.ds(0, (NT - 1) * R), :], t_sem)
 
     def mate(k):
         return copy(mate_send.at[k], mate_recv.at[k], mate_sem, k, at(dc=1))
 
     def r1a(k, i):
         return copy(
-            folded.at[k, :, mod(x + i, X), :, pl.ds(0, QUARTER)],
+            folded.at[k, :, mod(x + i, X), :, pl.ds(0, PA)],
             first_a.at[k, i - 1],
             r1a_sem,
-            k * X + i,
+            k,
             at(dx=i),
         )
 
     def r1b(k, i):
         return copy(
-            folded.at[k, mod(y + i, Y), :, :, pl.ds(QUARTER, QUARTER)],
+            folded.at[k, mod(y + i, Y), :, :, pl.ds(PA, PA)],
             first_b.at[k, i - 1],
             r1b_sem,
-            k * Y + i,
+            k,
             at(dy=i),
+        )
+
+    def r1c(k):
+        return copy(
+            folded.at[k, :, :, :, pl.ds(2 * PA, PC)], first_c.at[k], r1c_sem, 0, at(dz=k + 1)
         )
 
     loss_voc[voc] = jnp.zeros((8, LANES), F32)
@@ -479,6 +525,10 @@
         each(X, lambda i: r1a(k, i).start(), 1)
         each(Y, lambda i: r1b(k, i).start(), 1)
 
+        @pl.when(k < Z - 1)
+        def _():
+            r1c(k).start()
+
     def weight_part(b):
         wide = gathered[b // 2, mod(b, 2)].reshape(N, CS)
         value = lax.dot_general(
@@ -487,44 +537,55 @@
         grad_weight[pl.ds(pl.multiple_of(b * CS, CS), CS), :] = value.astype(BF16)
 
     def r2a(k, i):
-        return copy(
-            second_a.at[k, mod(y + i, Y)], got_a.at[k, i - 1], r2a_sem, k * Y + i, at(dy=i)
-        )
+        return copy(second_a.at[k, mod(y + i, Y)], got_a.at[k, i - 1], r2a_sem, k, at(dy=i))
 
     def r2b(k, i):
-        return copy(
-            second_b.at[k, mod(x + i, X)], got_b.at[k, i - 1], r2b_sem, k * X + i, at(dx=i)
-        )
+        return copy(second_b.at[k, mod(x + i, X)], got_b.at[k, i - 1], r2b_sem, k, at(dx=i))
+
+    def add(value, others):
+        for other in others:
+            value = value + other.astype(F32)
+        return value
 
     def fold_first(k):
-        each(X, lambda i: r1a(k, i).wait(), 1)
-        value = folded[k, :, x, :, :QUARTER].astype(F32)
-        for i in range(X - 1):
-            value = value + first_a[k, i].astype(F32)
-        second_a[k] = value.astype(BF16)
+        join(first_a.at[k], r1a_sem, k)
+        value = folded[k, :, x, :, :PA].astype(F32)
+        second_a[k] = add(value, [first_a[k, i] for i in range(X - 1)]).astype(BF16)
         each(Y, lambda i: r2a(k, i).start(), 1)
-        each(Y, lambda i: r1b(k, i).wait(), 1)
-        value = folded[k, y, :, :, QUARTER:].astype(F32)
-        for i in range(Y - 1):
-            value = value + first_b[k, i].astype(F32)
-        second_b[k] = value.astype(BF16)
+        join(first_b.at[k], r1b_sem, k)
+        value = folded[k, y, :, :, PA : 2 * PA].astype(F32)
+        second_b[k] = add(value, [first_b[k, i] for i in range(Y - 1)]).astype(BF16)
         each(X, lambda i: r2b(k, i).start(), 1)
 
     def fold_second(k):
-        each(Y, lambda i: r2a(k, i).wait(), 1)
-        each(X, lambda i: r2b(k, i).wait(), 1)
-        left = second_a[k, y].astype(F32)
-        for i in range(Y - 1):
-            left = left + got_a[k, i].astype(F32)
-        right = second_b[k, x].astype(F32)
-        for i in range(X - 1):
-            right = right + got_b[k, i].astype(F32)
+        join(got_a.at[k], r2a_sem, k)
+        join(got_b.at[k], r2b_sem, k)
+        left = add(second_a[k, y].astype(F32), [got_a[k, i] for i in range(Y - 1)])
+        right = add(second_b[k, x].astype(F32), [got_b[k, i] for i in range(X - 1)])
         last[0, k] = jnp.concatenate([left, right], axis=1).astype(BF16)
 
+    def r2c(i):
+        return copy(second_c.at[mod(y + i, Y)], got_c.at[i - 1], r2c_sem, 0, at(dy=i))
+
+    def r3c(i):
+        return copy(third_c.at[mod(x + i, X)], got_d.at[i - 1], r3c_sem, 0, at(dx=i))
+
+    def fold_first_c():
+        join(first_c, r1c_sem)
+        value = folded[Z - 1, :, :, :, 2 * PA :].astype(F32)
+        second_c[...] = add(value, [first_c[k] for k in range(Z - 1)]).astype(BF16)
+        each(Y, lambda i: r2c(i).start(), 1)
+
+    def fold_second_c():
+        join(got_c, r2c_sem)
+        value = second_c[y].astype(F32)
+        third_c[...] = add(value, [got_c[i] for i in range(Y - 1)]).astype(BF16)
+        each(X, lambda i: r3c(i).start(), 1)
+
     def r3(k):
-        return copy(last.at[0, k], last.at[1, k], r3_sem, k, at(dz=k + 1))
-
-    LAG1, LAG2 = 3, 5
+        return copy(last.at[0, k], last.at[1, k], r3_sem, 0, at(dz=k + 1))
+
+    LAG1, LAG2 = 3, 4
 
     def turn(j):
         @pl.when(j < Z)
@@ -534,18 +595,6 @@
         @pl.when((j >= 1) & (j < Z + 1))
         def _():
             fold_mate(j - 1)
-
-        @pl.when((j >= LAG1) & (j < Z + LAG1))
-        def _():
-            fold_first(j - LAG1)
-
-        @pl.when((j >= LAG2) & (j < Z + LAG2))
-        def _():
-            fold_second(j - LAG2)
-
-        @pl.when((j >= LAG2) & (j < Z + LAG2 - 1))
-        def _():
-            r3(j - LAG2).start()
 
         @pl.when(j == Z)
         def _():
@@ -559,6 +608,7 @@
 
         @pl.when(j == Z + 2)
         def _():
+            fold_first_c()
             loss_stages[1][1]()
             loss_z[z] = functools.reduce(jnp.add, [loss_y[i] for i in range(Y)])
             loss_stages[2][0]()
@@ -568,14 +618,31 @@
             weight_part(2 * (j - Z))
             weight_part(2 * (j - Z) + 1)
 
+        @pl.when((j >= LAG1) & (j < Z + LAG1))
+        def _():
+            fold_first(j - LAG1)
+
+        @pl.when(j == Z + 3)
+        def _():
+            fold_second_c()
+
+        @pl.when(j >= LAG2)
+        def _():
+            fold_second(j - LAG2)
+
+        @pl.when((j >= LAG2) & (j < Z + LAG2 - 1))
+        def _():
+            r3(j - LAG2).start()
+
     each(Z + LAG2, turn)
     loss_stages[2][1]()
     loss = functools.reduce(jnp.add, [loss_z[j] for j in range(Z)])
-    loss_out[...] = TEMPERATURE * TEMPERATURE * loss / (N - lengths.shape[0])
-    each(Z - 1, lambda k: r3(k).wait())
-    value = last[0, Z - 1].astype(F32)
-    for k in range(Z - 1):
-        value = value + last[1, k].astype(F32)
+    loss_out[0, 0] = jnp.max(TEMPERATURE * TEMPERATURE * loss / (N - lengths.shape[0]))
+    join(last.at[1, pl.ds(0, Z - 1)], r3_sem)
+    join(got_d, r3c_sem)
+    value = add(last[0, Z - 1].astype(F32), [last[1, k] for k in range(Z - 1)])
+    right = add(third_c[x].astype(F32), [got_d[i] for i in range(X - 1)])
+    value = jnp.concatenate([value, right], axis=1)
     final[...] = value
     swap = copy(final.at[pl.ds(pl.multiple_of((1 - core) * 8, 8), 8), :], final_recv, final_sem, 0, at(dc=1))
     swap.start()
@@ -589,7 +656,9 @@
 def body(dims, hidden, weights, mentor, rows, lengths):
     Z, Y, X, R, V, D = dims
     NT, NV, CH = Z * Y, X * 2, Y * R
-    N, HALF, QUARTER, CS = Z * CH, D // 2, D // 4, D // NV
+    N, HALF, CS = Z * CH, D // 2, D // NV
+    PC = HALF // 4
+    PA = (HALF - PC) // 2
     vmem = pl.BlockSpec(memory_space=pltpu.VMEM)
     anywhere = pl.BlockSpec(memory_space=pl.ANY)
     nb = max(1, CH // LANES)
@@ -598,16 +667,18 @@
     loss, grad_hidden, grad_weight = pl.pallas_call(
         functools.partial(kernel, dims),
         out_shape=(
-            jax.ShapeDtypeStruct((8, LANES), F32),
+            jax.ShapeDtypeStruct((1, 1), F32),
             jax.ShapeDtypeStruct((8, D), BF16),
             jax.ShapeDtypeStruct((D, V), BF16),
         ),
         in_specs=[anywhere, anywhere, anywhere, vmem, pl.BlockSpec(memory_space=pltpu.SMEM)],
-        out_specs=(vmem, vmem, vmem),
+        out_specs=(pl.BlockSpec(memory_space=pltpu.SMEM), vmem, vmem),
         scratch_shapes=[
             pltpu.VMEM((D, V), BF16),
             pltpu.VMEM((R, V * NT), BF16),
             pltpu.VMEM((N, 1), jnp.int32),
+            pltpu.VMEM((R, LANES), F32),
+            pltpu.VMEM((R, LANES), F32),
             pltpu.VMEM((X, 2, Z, Y, R, CS), BF16),
             pltpu.VMEM((N, V), BF16),
             pltpu.VMEM((N, N), BF16),
@@ -617,13 +688,18 @@
             pltpu.VMEM((Z, CH, HALF), BF16),
             pltpu.VMEM((2, CH, HALF), F32),
             pltpu.VMEM((Z, Y, X, 16, HALF), BF16),
-            pltpu.VMEM((Z, X - 1, Y, 16, QUARTER), BF16),
-            pltpu.VMEM((Z, Y - 1, X, 16, QUARTER), BF16),
-            pltpu.VMEM((Z, Y, 16, QUARTER), BF16),
-            pltpu.VMEM((Z, X, 16, QUARTER), BF16),
-            pltpu.VMEM((Z, Y - 1, 16, QUARTER), BF16),
-            pltpu.VMEM((Z, X - 1, 16, QUARTER), BF16),
-            pltpu.VMEM((2, Z, 16, HALF), BF16),
+            pltpu.VMEM((Z, X - 1, Y, 16, PA), BF16),
+            pltpu.VMEM((Z, Y - 1, X, 16, PA), BF16),
+            pltpu.VMEM((Z, Y, 16, PA), BF16),
+            pltpu.VMEM((Z, X, 16, PA), BF16),
+            pltpu.VMEM((Z, Y - 1, 16, PA), BF16),
+            pltpu.VMEM((Z, X - 1, 16, PA), BF16),
+            pltpu.VMEM((Z - 1, Y, X, 16, PC), BF16),
+            pltpu.VMEM((Y, X, 16, PC), BF16),
+            pltpu.VMEM((Y - 1, X, 16, PC), BF16),
+            pltpu.VMEM((X, 16, PC), BF16),
+            pltpu.VMEM((X - 1, 16, PC), BF16),
+            pltpu.VMEM((2, Z, 16, 2 * PA), BF16),
             pltpu.VMEM((16, HALF), F32),
             pltpu.VMEM((8, HALF), F32),
             pltpu.VMEM((NV, 2 * tiles, 8, LANES), F32),
@@ -637,34 +713,37 @@
             pltpu.VMEM((Z, 8, LANES), F32),
             pltpu.SemaphoreType.DMA((4,)),
             dma(Z),
-            dma(NT),
-            dma(Z * Y),
-            dma(Z * X),
-            dma(Z * X),
-            dma(Z * Y),
-            dma(Z),
-            dma(NV),
-            dma(Y),
-            dma(Z),
-            dma(NV),
-            dma(Y),
-            dma(Z),
-            dma(NV),
-            dma(Y),
-            dma(Z),
-            dma(Z),
-            dma(Z * X),
-            dma(Z * Y),
-            dma(Z * Y),
-            dma(Z * X),
-            dma(Z),
+            dma(1),
+            dma(Z),
+            dma(Z),
+            dma(Z),
+            dma(Z),
+            dma(Z),
+            dma(1),
+            dma(1),
+            dma(1),
+            dma(1),
+            dma(1),
+            dma(1),
+            dma(1),
+            dma(1),
+            dma(1),
+            dma(Z),
+            dma(Z),
+            dma(Z),
+            dma(Z),
+            dma(Z),
+            dma(1),
+            dma(1),
+            dma(1),
+            dma(1),
             dma(1),
         ],
         compiler_params=pltpu.CompilerParams(
             collective_id=0, has_side_effects=True, vmem_limit_bytes=63 * 2**20
         ),
     )(hidden, weights, mentor, rows.reshape(Z * nb, CH // nb), lengths)
-    return loss[0, 0], grad_hidden, grad_weight
+    return loss.reshape(()), grad_hidden, grad_weight
 
 
 def solution(mesh):

time: 146 us -> 144 us (0.986)
  Pallas kernels: 139 us -> 137 us
  between operations: 0.64 us -> 2.31 us
    pallas_call x1, Pallas kernels: 139 us -> 137 us  [body(): pl.pallas_call(functools.partial(kernel, dims), out_shape=(jax.ShapeDtype...]
where the time goes in v3:
time: 144 us
  Pallas kernels  137 us (95%)
  local copies, waits for them, and re-layouts  4.42 us (3%)
  between operations  2.31 us (2%)
    pallas_call x1, Pallas kernels, body(): pl.pallas_call(functools.partial(kernel, dims), out_shape=(jax.ShapeDtype...  137 us
    unnamed x2, local copies, waits for them, and re-layouts  4.42 us

profile of v3, /device:TPU:1, one launch (start us, length us, event | category | flops | bytes accessed | tf_op | source)
XLA Modules:
  0.0 143.8 jit_solution(8469943590616189088)
XLA Ops:
  0.6 137.1 %shard_map.76 = (f32[1,1]{1,0:T(1,128)}, bf16[8,2048]{1,0:T(8,128)(2,1)}, bf16[2048,512]{1,0:T(8,128)(2,1)}) custom-call(bf16[64,2048]{1,0:T(8,128)(2,1)} %hidden.1, bf16[2048,512]{1,0:T(8,128)(2,1)} %weights_hbm.1, bf16[64,16384]{1,0:T(8,128)(2,1)} %mentor_hbm.1, s32[16,128]{1,0:T(8,128)} %bitcast.2, s32[8]{0:T(128)} %lengths.1), custom_call_target="tpu_custom_call" | custom-call | tf_op jit(solution)/shard_map/pallas_call | solution.py:667
  138.3 1.4 copy.12
  139.7 3.0 %copy.13 = bf16[2048,512]{1,0:T(8,128)(2,1)} copy(bf16[2048,512]{1,0:T(8,128)(2,1)} %get-tuple-element.14) | data formatting | bytes 4194304

commit v4 on v3

--- a/solution.py
+++ b/solution.py
@@ -105,7 +105,7 @@
     PC = HALF // 4
     PA = (HALF - PC) // 2
     CS = D // NV
-    CP = CS // 2
+    RA = (3 * R // 4) // 16 * 16
     nb = max(1, CH // LANES)
     q = CH // nb
     per_tile = 8 // nb
@@ -287,7 +287,7 @@
             mentor_z[z, j] = mentor_y[j]
         mentor_stages[2][0]()
 
-    first, second = pl.ds(0, CP), pl.ds(CP, CP)
+    first, second = pl.ds(0, RA), pl.ds(RA, R - RA)
     stat_voc[voc] = jnp.zeros((2 * tiles, 8, LANES), F32)
 
     def away(j):
@@ -297,19 +297,19 @@
         return mod(z + Z - away(j), Z)
 
     def s2a(j, i):
-        block = gathered.at[x, core, chunk(j), y, :, first]
+        block = gathered.at[x, core, chunk(j), y, first]
         return copy(block, block, s2a_sem, j, at(dy=i))
 
     def s2b(j, i):
-        block = gathered.at[x, core, chunk(j), y, :, second]
+        block = gathered.at[x, core, chunk(j), y, second]
         return copy(block, block, s2b_sem, j, at(dx=i))
 
     def s3a(j, i):
-        block = gathered.at[x, core, chunk(j), :, :, first]
+        block = gathered.at[x, core, chunk(j), :, first]
         return copy(block, block, s3a_sem, j, at(dx=i))
 
     def s3b(j, i):
-        block = gathered.at[:, core, chunk(j), y, :, second]
+        block = gathered.at[:, core, chunk(j), y, second]
         return copy(block, block, s3b_sem, j, at(dy=i))
 
     def c(j):
@@ -336,61 +336,51 @@
         put(top, k // per_tile)
         put(total, tiles + k // per_tile)
 
-    def gather(j):
-        @pl.when(j == 0)
-        def _():
-            own_columns.wait()
-            load_mentor.wait()
-
-        @pl.when((j > 0) & (j < Z))
-        def _():
-            s1(away(j)).wait()
-
-        @pl.when(j < Z)
-        def _():
-            each(Y, lambda i: s2a(j, i).start(), 1)
-            each(X, lambda i: s2b(j, i).start(), 1)
-
-        @pl.when((j >= 1) & (j < Z + 1))
-        def _():
-            join(gathered.at[x, core, chunk(j - 1), pl.ds(0, Y - 1), :, first], s2a_sem, j - 1)
-            each(X, lambda i: s3a(j - 1, i).start(), 1)
-            join(gathered.at[pl.ds(0, X - 1), core, chunk(j - 1), y, :, second], s2b_sem, j - 1)
-            each(Y, lambda i: s3b(j - 1, i).start(), 1)
-
-        @pl.when((j >= 2) & (j < Z + 2))
-        def _():
-            join(gathered.at[pl.ds(0, X - 1), core, chunk(j - 2), :, :, first], s3a_sem, j - 2)
-            join(gathered.at[:, core, chunk(j - 2), pl.ds(0, Y - 1), :, second], s3b_sem, j - 2)
-            c(j - 2).start()
-
-        @pl.when(j < Z)
-        def _():
-            mentor_part(j)
-            fill_picks(j)
-
-        @pl.when(j == Z - 1)
-        def _():
-            mentor_done()
-
-        @pl.when(j == Z)
-        def _():
-            mentor_second()
-
-        @pl.when(j == Z + 1)
-        def _():
-            mentor_third()
-
-        @pl.when(j == 3)
-        def _():
-            load_weights.wait()
-
-        @pl.when(j >= 3)
-        def _():
-            c(j - 3).wait()
-            score(chunk(j - 3))
-
-    each(Z + 3, gather)
+    def second_step(j):
+        each(Y, lambda i: s2a(j, i).start(), 1)
+        each(X, lambda i: s2b(j, i).start(), 1)
+
+    def third_step(j):
+        join(gathered.at[x, core, chunk(j), pl.ds(0, Y - 1), first], s2a_sem, j)
+        each(X, lambda i: s3a(j, i).start(), 1)
+        join(gathered.at[pl.ds(0, X - 1), core, chunk(j), y, second], s2b_sem, j)
+        each(Y, lambda i: s3b(j, i).start(), 1)
+
+    def fourth_step(j):
+        join(gathered.at[pl.ds(0, X - 1), core, chunk(j), :, first], s3a_sem, j)
+        join(gathered.at[:, core, chunk(j), pl.ds(0, Y - 1), second], s3b_sem, j)
+        c(j).start()
+
+    def last_step(j):
+        c(j).wait()
+        score(chunk(j))
+
+    own_columns.wait()
+    second_step(0)
+    load_mentor.wait()
+    each(Z // 2, mentor_part)
+    third_step(0)
+    each(Z, mentor_part, Z // 2)
+    mentor_done()
+
+    def on_first(j):
+        s1(away(j)).wait()
+        second_step(j)
+
+    each(Z, on_first, 1)
+    each(Z, third_step, 1)
+    mentor_second()
+    each(Z, fill_picks)
+    mentor_third()
+    load_weights.wait()
+    fourth_step(0)
+
+    def on_third(j):
+        fourth_step(j)
+        last_step(j - 1)
+
+    each(Z, on_third, 1)
+    last_step(Z - 1)
 
     def combine(buf, n):
         tops = [buf[j, :tiles] for j in range(n)]
@@ -585,56 +575,56 @@
     def r3(k):
         return copy(last.at[0, k], last.at[1, k], r3_sem, 0, at(dz=k + 1))
 
-    LAG1, LAG2 = 3, 4
-
-    def turn(j):
+    def forward(j):
         @pl.when(j < Z)
         def _():
             gradient(j)
 
-        @pl.when((j >= 1) & (j < Z + 1))
+        @pl.when(j >= 1)
         def _():
             fold_mate(j - 1)
 
-        @pl.when(j == Z)
-        def _():
-            loss_stages[0][0]()
-
-        @pl.when(j == Z + 1)
+    each(Z + 1, forward)
+    loss_stages[0][0]()
+    PER = NV // Z if NV > Z else 1
+    LAG = 2
+
+    def backward(j):
+        @pl.when(j < Z)
+        def _():
+            fold_first(j)
+            for i in range(PER):
+                weight_part(j * PER + i)
+
+        @pl.when(j == 1)
         def _():
             loss_stages[0][1]()
             loss_y[y] = functools.reduce(jnp.add, [loss_voc[i] for i in range(NV)])
             loss_stages[1][0]()
 
-        @pl.when(j == Z + 2)
-        def _():
-            fold_first_c()
+        @pl.when(j == Z - 3)
+        def _():
             loss_stages[1][1]()
             loss_z[z] = functools.reduce(jnp.add, [loss_y[i] for i in range(Y)])
             loss_stages[2][0]()
 
-        @pl.when((j >= Z) & (j < Z + NV // 2))
-        def _():
-            weight_part(2 * (j - Z))
-            weight_part(2 * (j - Z) + 1)
-
-        @pl.when((j >= LAG1) & (j < Z + LAG1))
-        def _():
-            fold_first(j - LAG1)
-
-        @pl.when(j == Z + 3)
+        @pl.when(j == Z - 1)
+        def _():
+            fold_first_c()
+
+        @pl.when(j == Z)
         def _():
             fold_second_c()
 
-        @pl.when(j >= LAG2)
-        def _():
-            fold_second(j - LAG2)
-
-        @pl.when((j >= LAG2) & (j < Z + LAG2 - 1))
-        def _():
-            r3(j - LAG2).start()
-
-    each(Z + LAG2, turn)
+        @pl.when(j >= LAG)
+        def _():
+            fold_second(j - LAG)
+
+        @pl.when((j >= LAG) & (j < Z + LAG - 1))
+        def _():
+            r3(j - LAG).start()
+
+    each(Z + LAG, backward)
     loss_stages[2][1]()
     loss = functools.reduce(jnp.add, [loss_z[j] for j in range(Z)])
     loss_out[0, 0] = jnp.max(TEMPERATURE * TEMPERATURE * loss / (N - lengths.shape[0]))

time: 144 us -> 134 us (0.931)
  Pallas kernels: 137 us -> 127 us
    pallas_call x1, Pallas kernels: 137 us -> 127 us  [body(): pl.pallas_call(functools.partial(kernel, dims), out_shape=(jax.ShapeDtype...]
where the time goes in v4:
time: 134 us
  Pallas kernels  127 us (95%)
  local copies, waits for them, and re-layouts  4.42 us (3%)
  between operations  2.31 us (2%)
    pallas_call x1, Pallas kernels, body(): pl.pallas_call(functools.partial(kernel, dims), out_shape=(jax.ShapeDtype...  127 us
    unnamed x2, local copies, waits for them, and re-layouts  4.42 us

profile of v4, /device:TPU:1, one launch (start us, length us, event | category | flops | bytes accessed | tf_op | source)
XLA Modules:
  0.0 133.6 jit_solution(2642080030990564930)
XLA Ops:
  0.6 126.9 %shard_map.76 = (f32[1,1]{1,0:T(1,128)}, bf16[8,2048]{1,0:T(8,128)(2,1)}, bf16[2048,512]{1,0:T(8,128)(2,1)}) custom-call(bf16[64,2048]{1,0:T(8,128)(2,1)} %hidden.1, bf16[2048,512]{1,0:T(8,128)(2,1)} %weights_hbm.1, bf16[64,16384]{1,0:T(8,128)(2,1)} %mentor_hbm.1, s32[16,128]{1,0:T(8,128)} %bitcast.2, s32[8]{0:T(128)} %lengths.1), custom_call_target="tpu_custom_call" | custom-call | tf_op jit(solution)/shard_map/pallas_call | solution.py:657
  128.0 1.4 %copy.12 = bf16[8,2048]{1,0:T(8,128)(2,1)} copy(bf16[8,2048]{1,0:T(8,128)(2,1)} %get-tuple-element.13) | data formatting | bytes 65536
  129.4 3.0 %copy.13 = bf16[2048,512]{1,0:T(8,128)(2,1)} copy(bf16[2048,512]{1,0:T(8,128)(2,1)} %get-tuple-element.14) | data formatting | bytes 4194304

commit v5 on v4

--- a/solution.py
+++ b/solution.py
@@ -142,6 +142,9 @@
     load_mentor.start()
     load_weights.start()
 
+    def turns(i, n):
+        return jnp.where(mod(i, 2) == 1, n // 2 - (i + 1) // 2, n // 2 + i // 2)
+
     barrier = pltpu.get_barrier_semaphore()
 
     def greet_tok(i):
@@ -163,7 +166,7 @@
             at(dz=i),
         )
 
-    each(Z, lambda i: s1(i).start(), 1)
+    each(Z - 1, lambda i: s1(turns(i, Z)).start())
     own_columns = pltpu.make_async_copy(
         hidden.at[:, pl.ds(pl.multiple_of(voc * CS, CS), CS)],
         gathered.at[x, core, z, y],
@@ -172,7 +175,7 @@
     own_columns.start()
 
     def t_copy(i):
-        device = at(dz=i // Y, dy=mod(i, Y))
+        device = at(dz=turns(i // Y, Z), dy=turns(mod(i, Y), Y))
         return copy(
             mentor_hbm.at[:, pl.ds(pl.multiple_of(device[0] * V, V), V)],
             teacher.at[pl.ds(pl.multiple_of(tok * R, R), R), :],
@@ -181,7 +184,7 @@
             device,
         )
 
-    each(NT, lambda i: t_copy(i).start(), 1)
+    each(NT - 1, lambda i: t_copy(i).start())
     own_block = pltpu.make_async_copy(
         mentor_hbm.at[:, pl.ds(pl.multiple_of(tok * V, V), V)],
         teacher.at[pl.ds(pl.multiple_of(tok * R, R), R), :],
@@ -291,7 +294,7 @@
     stat_voc[voc] = jnp.zeros((2 * tiles, 8, LANES), F32)
 
     def away(j):
-        return mod(jnp.where(mod(j, 2) == 1, (j + 1) // 2, Z - j // 2), Z)
+        return turns(mod(j + Z - 1, Z), Z)
 
     def chunk(j):
         return mod(z + Z - away(j), Z)
@@ -448,13 +451,13 @@
 
     def r1c(k):
         return copy(
-            folded.at[k, :, :, :, pl.ds(2 * PA, PC)], first_c.at[k], r1c_sem, 0, at(dz=k + 1)
+            folded.at[k, :, :, :, pl.ds(2 * PA, PC)], first_c.at[k], r1c_sem, 0, at(dz=turns(k, Z))
         )
 
     loss_voc[voc] = jnp.zeros((8, LANES), F32)
 
     def gradient(k):
-        zc = mod(z + 1 + k, Z)
+        zc = mod(z + turns(k, Z), Z)
         here = pl.ds(pl.multiple_of(zc * CH, CH), CH)
         wanted = wanted_rows[here, :]
         block = wanted // R
@@ -573,7 +576,7 @@
         each(X, lambda i: r3c(i).start(), 1)
 
     def r3(k):
-        return copy(last.at[0, k], last.at[1, k], r3_sem, 0, at(dz=k + 1))
+        return copy(last.at[0, k], last.at[1, k], r3_sem, 0, at(dz=turns(k, Z)))
 
     def forward(j):
         @pl.when(j < Z)

time: 134 us -> 125 us (0.933)
  Pallas kernels: 127 us -> 118 us
    pallas_call x1, Pallas kernels: 127 us -> 118 us  [body(): pl.pallas_call(functools.partial(kernel, dims), out_shape=(jax.ShapeDtype...]
where the time goes in v5:
time: 125 us
  Pallas kernels  118 us (94%)
  local copies, waits for them, and re-layouts  4.42 us (4%)
  between operations  2.31 us (2%)
    pallas_call x1, Pallas kernels, body(): pl.pallas_call(functools.partial(kernel, dims), out_shape=(jax.ShapeDtype...  118 us
    unnamed x2, local copies, waits for them, and re-layouts  4.42 us

profile of v5, /device:TPU:1, one launch (start us, length us, event | category | flops | bytes accessed | tf_op | source)
XLA Modules:
  0.0 124.9 jit_solution(5950223136230870854)
XLA Ops:
  0.6 118.2 %shard_map.76 = (f32[1,1]{1,0:T(1,128)}, bf16[8,2048]{1,0:T(8,128)(2,1)}, bf16[2048,512]{1,0:T(8,128)(2,1)}) custom-call(bf16[64,2048]{1,0:T(8,128)(2,1)} %hidden.1, bf16[2048,512]{1,0:T(8,128)(2,1)} %weights_hbm.1, bf16[64,16384]{1,0:T(8,128)(2,1)} %mentor_hbm.1, s32[16,128]{1,0:T(8,128)} %bitcast.2, s32[8]{0:T(128)} %lengths.1), custom_call_target="tpu_custom_call" | custom-call | tf_op jit(solution)/shard_map/pallas_call | solution.py:660
  119.4 1.4 %copy.12 = bf16[8,2048]{1,0:T(8,128)(2,1)} copy(bf16[8,2048]{1,0:T(8,128)(2,1)} %get-tuple-element.13) | data formatting | bytes 65536
  120.8 3.0 %copy.13 = bf16[2048,512]{1,0:T(8,128)(2,1)} copy(bf16[2048,512]{1,0:T(8,128)(2,1)} %get-tuple-element.14) | data formatting | bytes 4194304

commit v6 on v5

--- a/solution.py
+++ b/solution.py
@@ -28,6 +28,7 @@
     lengths,
     loss_out,
     grad_hidden,
+    grad_weight_hbm,
     grad_weight,
     weights,
     mentor,
@@ -55,8 +56,7 @@
     third_c,
     got_d,
     last,
-    final,
-    final_recv,
+    arrived,
     stat_voc,
     stat_y,
     stat_z,
@@ -92,7 +92,6 @@
     r2c_sem,
     r3c_sem,
     r3_sem,
-    final_sem,
 ):
     Z, Y, X, R, V, D = dims
     tok, voc = lax.axis_index("tok"), lax.axis_index("voc")
@@ -153,9 +152,13 @@
     def greet_voc(i):
         pl.semaphore_signal(barrier, inc=1, device_id=at(dx=i // 2, dc=mod(i, 2)), device_id_type=MESH)
 
+    def greet_cross(i):
+        pl.semaphore_signal(barrier, inc=1, device_id=at(dz=i, dc=1), device_id_type=MESH)
+
     each(NT, greet_tok, 1)
     each(NV, greet_voc, 1)
-    pl.semaphore_wait(barrier, NT - 1 + NV - 1)
+    each(Z, greet_cross, 1)
+    pl.semaphore_wait(barrier, NT - 1 + NV - 1 + Z - 1)
 
     def s1(i):
         return copy(
@@ -184,7 +187,6 @@
             device,
         )
 
-    each(NT - 1, lambda i: t_copy(i).start())
     own_block = pltpu.make_async_copy(
         mentor_hbm.at[:, pl.ds(pl.multiple_of(tok * V, V), V)],
         teacher.at[pl.ds(pl.multiple_of(tok * R, R), R), :],
@@ -360,6 +362,7 @@
 
     own_columns.wait()
     second_step(0)
+    each(NT - 1, lambda i: t_copy(i).start())
     load_mentor.wait()
     each(Z // 2, mentor_part)
     third_step(0)
@@ -555,13 +558,22 @@
         join(got_b.at[k], r2b_sem, k)
         left = add(second_a[k, y].astype(F32), [got_a[k, i] for i in range(Y - 1)])
         right = add(second_b[k, x].astype(F32), [got_b[k, i] for i in range(X - 1)])
-        last[0, k] = jnp.concatenate([left, right], axis=1).astype(BF16)
+        for d in range(2):
+            rows8 = slice(8 * d, 8 * d + 8)
+            last[k, d] = jnp.concatenate([left[rows8], right[rows8]], axis=0).astype(BF16)
 
     def r2c(i):
         return copy(second_c.at[mod(y + i, Y)], got_c.at[i - 1], r2c_sem, 0, at(dy=i))
 
     def r3c(i):
-        return copy(third_c.at[mod(x + i, X)], got_d.at[i - 1], r3c_sem, 0, at(dx=i))
+        dx, dc = i // 2, mod(i, 2)
+        return copy(
+            third_c.at[mod(x + dx, X), mod(core + dc, 2)],
+            got_d.at[2 * dx + core],
+            r3c_sem,
+            0,
+            at(dx=dx, dc=dc),
+        )
 
     def fold_first_c():
         join(first_c, r1c_sem)
@@ -572,11 +584,23 @@
     def fold_second_c():
         join(got_c, r2c_sem)
         value = second_c[y].astype(F32)
-        third_c[...] = add(value, [got_c[i] for i in range(Y - 1)]).astype(BF16)
-        each(X, lambda i: r3c(i).start(), 1)
-
-    def r3(k):
-        return copy(last.at[0, k], last.at[1, k], r3_sem, 0, at(dz=turns(k, Z)))
+        value = add(value, [got_c[i] for i in range(Y - 1)])
+        for i in range(X):
+            for d in range(2):
+                part = value[i, 8 * d : 8 * d + 8]
+                part = jnp.concatenate([part[:, : PC // 2], part[:, PC // 2 :]], axis=0)
+                third_c[i, d] = part.astype(BF16)
+        each(NV, lambda i: r3c(i).start(), 1)
+        got_d[core] = third_c[x, core]
+
+    def r3(k, dc):
+        return copy(
+            last.at[k, mod(core + dc, 2)],
+            arrived.at[2 * k + core],
+            r3_sem,
+            0,
+            at(dz=turns(k, Z), dc=dc),
+        )
 
     def forward(j):
         @pl.when(j < Z)
@@ -589,61 +613,57 @@
 
     each(Z + 1, forward)
     loss_stages[0][0]()
-    PER = NV // Z if NV > Z else 1
+    PER = NV // (Z // 2)
     LAG = 2
 
     def backward(j):
-        @pl.when(j < Z)
+        fold_first(j)
+
+        @pl.when(j < Z // 2)
         def _():
-            fold_first(j)
             for i in range(PER):
                 weight_part(j * PER + i)
 
-        @pl.when(j == 1)
+        @pl.when(j == Z // 2 - 1)
         def _():
             loss_stages[0][1]()
             loss_y[y] = functools.reduce(jnp.add, [loss_voc[i] for i in range(NV)])
             loss_stages[1][0]()
 
-        @pl.when(j == Z - 3)
+        @pl.when(j == Z - 2)
         def _():
             loss_stages[1][1]()
             loss_z[z] = functools.reduce(jnp.add, [loss_y[i] for i in range(Y)])
             loss_stages[2][0]()
 
-        @pl.when(j == Z - 1)
-        def _():
-            fold_first_c()
-
-        @pl.when(j == Z)
-        def _():
-            fold_second_c()
-
         @pl.when(j >= LAG)
         def _():
             fold_second(j - LAG)
-
-        @pl.when((j >= LAG) & (j < Z + LAG - 1))
-        def _():
-            r3(j - LAG).start()
-
-    each(Z + LAG, backward)
+            r3(j - LAG, 0).start()
+            r3(j - LAG, 1).start()
+
+    each(Z, backward)
+    fold_first_c()
+    store_weight = pltpu.make_async_copy(grad_weight, grad_weight_hbm, local_sem.at[0])
+    store_weight.start()
+    fold_second(Z - 2)
+    r3(Z - 2, 0).start()
+    r3(Z - 2, 1).start()
+    fold_second(Z - 1)
+    r3(Z - 1, 1).start()
+    arrived[2 * (Z - 1) + core] = last[Z - 1, core]
+    fold_second_c()
     loss_stages[2][1]()
     loss = functools.reduce(jnp.add, [loss_z[j] for j in range(Z)])
     loss_out[0, 0] = jnp.max(TEMPERATURE * TEMPERATURE * loss / (N - lengths.shape[0]))
-    join(last.at[1, pl.ds(0, Z - 1)], r3_sem)
-    join(got_d, r3c_sem)
-    value = add(last[0, Z - 1].astype(F32), [last[1, k] for k in range(Z - 1)])
-    right = add(third_c[x].astype(F32), [got_d[i] for i in range(X - 1)])
-    value = jnp.concatenate([value, right], axis=1)
-    final[...] = value
-    swap = copy(final.at[pl.ds(pl.multiple_of((1 - core) * 8, 8), 8), :], final_recv, final_sem, 0, at(dc=1))
-    swap.start()
-    mine = jnp.where(core == 0, value[:8], value[8:])
-    swap.wait()
-    theirs = final_recv[...]
-    grad_hidden[:, :HALF] = jnp.where(core == 0, mine, theirs).astype(BF16)
-    grad_hidden[:, HALF:] = jnp.where(core == 0, theirs, mine).astype(BF16)
+    join(arrived.at[pl.ds(0, 2 * Z - 1)], r3_sem)
+    join(got_d.at[pl.ds(0, NV - 1)], r3c_sem)
+    for d in range(2):
+        value = add(arrived[d].astype(F32), [arrived[2 * k + d] for k in range(1, Z)])
+        right = add(got_d[d].astype(F32), [got_d[2 * i + d] for i in range(1, X)])
+        parts = [value[:8], value[8:], right[:8], right[8:]]
+        grad_hidden[:, d * HALF : (d + 1) * HALF] = jnp.concatenate(parts, axis=1).astype(BF16)
+    store_weight.wait()
 
 
 def body(dims, hidden, weights, mentor, rows, lengths):
@@ -665,8 +685,9 @@
             jax.ShapeDtypeStruct((D, V), BF16),
         ),
         in_specs=[anywhere, anywhere, anywhere, vmem, pl.BlockSpec(memory_space=pltpu.SMEM)],
-        out_specs=(pl.BlockSpec(memory_space=pltpu.SMEM), vmem, vmem),
+        out_specs=(pl.BlockSpec(memory_space=pltpu.SMEM), vmem, anywhere),
         scratch_shapes=[
+            pltpu.VMEM((D, V), BF16),
             pltpu.VMEM((D, V), BF16),
             pltpu.VMEM((R, V * NT), BF16),
             pltpu.VMEM((N, 1), jnp.int32),
@@ -690,11 +711,10 @@
             pltpu.VMEM((Z - 1, Y, X, 16, PC), BF16),
             pltpu.VMEM((Y, X, 16, PC), BF16),
             pltpu.VMEM((Y - 1, X, 16, PC), BF16),
-            pltpu.VMEM((X, 16, PC), BF16),
-            pltpu.VMEM((X - 1, 16, PC), BF16),
-            pltpu.VMEM((2, Z, 16, 2 * PA), BF16),
-            pltpu.VMEM((16, HALF), F32),
-            pltpu.VMEM((8, HALF), F32),
+            pltpu.VMEM((X, 2, 16, PC // 2), BF16),
+            pltpu.VMEM((NV, 16, PC // 2), BF16),
+            pltpu.VMEM((Z, 2, 16, PA), BF16),
+            pltpu.VMEM((2 * Z, 16, PA), BF16),
             pltpu.VMEM((NV, 2 * tiles, 8, LANES), F32),
             pltpu.VMEM((Y, 2 * tiles, 8, LANES), F32),
             pltpu.VMEM((Z, 2 * tiles, 8, LANES), F32),
@@ -730,7 +750,6 @@
             dma(1),
             dma(1),
             dma(1),
-            dma(1),
         ],
         compiler_params=pltpu.CompilerParams(
             collective_id=0, has_side_effects=True, vmem_limit_bytes=63 * 2**20

time: 125 us -> 121 us (0.968)
  Pallas kernels: 118 us -> 114 us
    pallas_call x1, Pallas kernels: 118 us -> 114 us  [body(): pl.pallas_call(functools.partial(kernel, dims), out_shape=(jax.ShapeDtype...]
where the time goes in v6:
time: 121 us
  Pallas kernels  114 us (94%)
  local copies, waits for them, and re-layouts  4.42 us (4%)
  between operations  2.31 us (2%)
    pallas_call x1, Pallas kernels, body(): pl.pallas_call(functools.partial(kernel, dims), out_shape=(jax.ShapeDtype...  114 us
    unnamed x2, local copies, waits for them, and re-layouts  4.42 us

profile of v6, /device:TPU:1, one launch (start us, length us, event | category | flops | bytes accessed | tf_op | source)
XLA Modules:
  0.0 120.7 jit_solution(18342494835362041911)
XLA Ops:
  0.6 114.0 %shard_map.76 = (f32[1,1]{1,0:T(1,128)}, bf16[8,2048]{1,0:T(8,128)(2,1)}, bf16[2048,512]{1,0:T(8,128)(2,1)}) custom-call(bf16[64,2048]{1,0:T(8,128)(2,1)} %hidden.1, bf16[2048,512]{1,0:T(8,128)(2,1)} %weights_hbm.1, bf16[64,16384]{1,0:T(8,128)(2,1)} %mentor_hbm.1, s32[16,128]{1,0:T(8,128)} %bitcast.2, s32[8]{0:T(128)} %lengths.1), custom_call_target="tpu_custom_call" | custom-call | tf_op jit(solution)/shard_map/pallas_call | solution.py:680
  115.2 1.4 %copy.12 = bf16[8,2048]{1,0:T(8,128)(2,1)} copy(bf16[8,2048]{1,0:T(8,128)(2,1)} %get-tuple-element.13) | data formatting | bytes 65536
  116.6 3.0 %copy.13 = bf16[2048,512]{1,0:T(8,128)(2,1)} copy(bf16[2048,512]{1,0:T(8,128)(2,1)} %get-tuple-element.14) | data formatting | bytes 4194304

commit v7 on v6

--- a/solution.py
+++ b/solution.py
@@ -28,7 +28,6 @@
     lengths,
     loss_out,
     grad_hidden,
-    grad_weight_hbm,
     grad_weight,
     weights,
     mentor,
@@ -39,6 +38,9 @@
     teacher,
     picks,
     scores,
+    mentor_top,
+    mentor_log,
+    weight_of,
     slope,
     mate_send,
     mate_recv,
@@ -417,16 +419,41 @@
     rest = table_log - log_hi.astype(F32)
     log_mid = rest.astype(BF16)
     log_lo = (rest - log_mid.astype(F32)).astype(BF16)
-    stat_stages[2][1]()
-    top_s, sum_s = combine(stat_z, Z)
-    stat_voc[0, :tiles] = top_s
-    stat_voc[0, tiles:] = jnp.log(jnp.where(sum_s > 0.0, sum_s, 1.0))
 
     ends = []
     total = jnp.int32(0)
     for j in range(lengths.shape[0]):
         total = total + lengths[j]
         ends.append(total - 1)
+
+    def prepare(k):
+        here = pl.ds(pl.multiple_of(k * CH, CH), CH)
+        wanted = wanted_rows[here, :]
+        block = wanted // R
+        pick = (lax.broadcasted_iota(jnp.int32, (CH, NT), 1) == block).astype(F32).astype(BF16)
+        lane = lax.broadcasted_iota(jnp.int32, (CH, LANES), 1) == (wanted - block * R)
+
+        def take(table):
+            return jnp.dot(pick, table, preferred_element_type=F32)
+
+        def one(value):
+            return jnp.sum(jnp.where(lane, value, 0.0), axis=1, keepdims=True)
+
+        teacher_top = one(take(table_top))
+        teacher_log = one(take(log_hi) + take(log_mid) + take(log_lo))
+        place = lax.broadcasted_iota(jnp.int32, (CH, 1), 0) + k * CH
+        valid = jnp.ones((CH, 1), F32)
+        for end in ends:
+            valid = jnp.where(place == end, 0.0, valid)
+        mentor_top[here, :] = teacher_top
+        mentor_log[here, :] = teacher_log
+        weight_of[here, :] = valid
+
+    each(Z, prepare)
+    stat_stages[2][1]()
+    top_s, sum_s = combine(stat_z, Z)
+    stat_voc[0, :tiles] = top_s
+    stat_voc[0, tiles:] = jnp.log(jnp.where(sum_s > 0.0, sum_s, 1.0))
 
     own_block.wait()
     join(teacher.at[pl.ds(0, (NT - 1) * R), :], t_sem)
@@ -462,19 +489,6 @@
     def gradient(k):
         zc = mod(z + turns(k, Z), Z)
         here = pl.ds(pl.multiple_of(zc * CH, CH), CH)
-        wanted = wanted_rows[here, :]
-        block = wanted // R
-        pick = (lax.broadcasted_iota(jnp.int32, (CH, NT), 1) == block).astype(F32).astype(BF16)
-        lane = lax.broadcasted_iota(jnp.int32, (CH, LANES), 1) == (wanted - block * R)
-
-        def take(table):
-            return jnp.dot(pick, table, preferred_element_type=F32)
-
-        def one(value):
-            return jnp.sum(jnp.where(lane, value, 0.0), axis=1, keepdims=True)
-
-        teacher_top = one(take(table_top))
-        teacher_log = one(take(log_hi) + take(log_mid) + take(log_lo))
         row_of = lax.broadcasted_iota(jnp.int32, (8, LANES), 0)
 
         def student(tile):
@@ -488,12 +502,9 @@
 
         student_top = student(0)
         student_log = student(tiles)
-        place = lax.broadcasted_iota(jnp.int32, (CH, 1), 0) + zc * CH
-        valid = jnp.ones((CH, 1), F32)
-        for end in ends:
-            valid = jnp.where(place == end, 0.0, valid)
+        valid = weight_of[here, :]
         taken = jnp.dot(picks[here, :], teacher[...], preferred_element_type=F32) / TEMPERATURE
-        log_teacher = (taken - teacher_top) - teacher_log
+        log_teacher = (taken - mentor_top[here, :]) - mentor_log[here, :]
         log_student = (scores[here, :] - student_top) - student_log
         p_teacher = jnp.exp(log_teacher)
         p_student = jnp.exp(log_student)
@@ -518,19 +529,20 @@
         mate(k).wait()
         value = own_half[mod(k, 2)] + mate_recv[k].astype(F32)
         folded[k] = value.astype(BF16).reshape(Y, X, 16, HALF)
-        each(X, lambda i: r1a(k, i).start(), 1)
-        each(Y, lambda i: r1b(k, i).start(), 1)
-
         @pl.when(k < Z - 1)
         def _():
             r1c(k).start()
+
+        each(X, lambda i: r1a(k, i).start(), 1)
+        each(Y, lambda i: r1b(k, i).start(), 1)
 
     def weight_part(b):
         wide = gathered[b // 2, mod(b, 2)].reshape(N, CS)
         value = lax.dot_general(
             wide, slope[...], (((0,), (0,)), ((), ())), preferred_element_type=F32
         )
-        grad_weight[pl.ds(pl.multiple_of(b * CS, CS), CS), :] = value.astype(BF16)
+        here = pl.ds(pl.multiple_of(b * CS, CS), CS)
+        grad_weight[here, :] = value.astype(BF16)
 
     def r2a(k, i):
         return copy(second_a.at[k, mod(y + i, Y)], got_a.at[k, i - 1], r2a_sem, k, at(dy=i))
@@ -613,7 +625,7 @@
 
     each(Z + 1, forward)
     loss_stages[0][0]()
-    PER = NV // (Z // 2)
+    PER = NV // Z
     LAG = 2
 
     def backward(j):
@@ -644,8 +656,7 @@
 
     each(Z, backward)
     fold_first_c()
-    store_weight = pltpu.make_async_copy(grad_weight, grad_weight_hbm, local_sem.at[0])
-    store_weight.start()
+    each(3 * NV // 4, weight_part, NV // 2)
     fold_second(Z - 2)
     r3(Z - 2, 0).start()
     r3(Z - 2, 1).start()
@@ -653,6 +664,7 @@
     r3(Z - 1, 1).start()
     arrived[2 * (Z - 1) + core] = last[Z - 1, core]
     fold_second_c()
+    each(NV, weight_part, 3 * NV // 4)
     loss_stages[2][1]()
     loss = functools.reduce(jnp.add, [loss_z[j] for j in range(Z)])
     loss_out[0, 0] = jnp.max(TEMPERATURE * TEMPERATURE * loss / (N - lengths.shape[0]))
@@ -663,7 +675,6 @@
         right = add(got_d[d].astype(F32), [got_d[2 * i + d] for i in range(1, X)])
         parts = [value[:8], value[8:], right[:8], right[8:]]
         grad_hidden[:, d * HALF : (d + 1) * HALF] = jnp.concatenate(parts, axis=1).astype(BF16)
-    store_weight.wait()
 
 
 def body(dims, hidden, weights, mentor, rows, lengths):
@@ -681,13 +692,12 @@
         functools.partial(kernel, dims),
         out_shape=(
             jax.ShapeDtypeStruct((1, 1), F32),
-            jax.ShapeDtypeStruct((8, D), BF16),
-            jax.ShapeDtypeStruct((D, V), BF16),
+            pltpu.VMEM((8, D), BF16),
+            pltpu.VMEM((D, V), BF16),
         ),
         in_specs=[anywhere, anywhere, anywhere, vmem, pl.BlockSpec(memory_space=pltpu.SMEM)],
-        out_specs=(pl.BlockSpec(memory_space=pltpu.SMEM), vmem, anywhere),
+        out_specs=(pl.BlockSpec(memory_space=pltpu.SMEM), vmem, vmem),
         scratch_shapes=[
-            pltpu.VMEM((D, V), BF16),
             pltpu.VMEM((D, V), BF16),
             pltpu.VMEM((R, V * NT), BF16),
             pltpu.VMEM((N, 1), jnp.int32),
@@ -697,6 +707,9 @@
             pltpu.VMEM((N, V), BF16),
             pltpu.VMEM((N, N), BF16),
             pltpu.VMEM((N, V), F32),
+            pltpu.VMEM((N, 1), F32),
+            pltpu.VMEM((N, 1), F32),
+            pltpu.VMEM((N, 1), F32),
             pltpu.VMEM((N, V), BF16),
             pltpu.VMEM((Z, CH, HALF), BF16),
             pltpu.VMEM((Z, CH, HALF), BF16),
@@ -752,7 +765,7 @@
             dma(1),
         ],
         compiler_params=pltpu.CompilerParams(
-            collective_id=0, has_side_effects=True, vmem_limit_bytes=63 * 2**20
+            collective_id=0, has_side_effects=True, vmem_limit_bytes=57 * 2**20
         ),
     )(hidden, weights, mentor, rows.reshape(Z * nb, CH // nb), lengths)
     return loss.reshape(()), grad_hidden, grad_weight

time: 121 us -> 118 us (0.975)
  local copies, waits for them, and re-layouts: 4.42 us -> 1.94 us
    unnamed x2, local copies, waits for them, and re-layouts: 4.42 us -> 1.94 us
where the time goes in v7:
time: 118 us
  Pallas kernels  113 us (96%)
  between operations  2.33 us (2%)
  local copies, waits for them, and re-layouts  1.94 us (2%)
    pallas_call x1, Pallas kernels, body(): pl.pallas_call(functools.partial(kernel, dims), out_shape=(jax.ShapeDtype...  113 us

profile of v7, /device:TPU:1, one launch (start us, length us, event | category | flops | bytes accessed | tf_op | source)
XLA Modules:
  0.0 117.7 jit_solution(8572283611516824982)
XLA Ops:
  0.6 113.5 %shard_map.76 = (f32[1,1]{1,0:T(1,128)}, bf16[8,2048]{1,0:T(8,128)(2,1)S(1)}, bf16[2048,512]{1,0:T(8,128)(2,1)S(1)}) custom-call(bf16[64,2048]{1,0:T(8,128)(2,1)} %hidden.1, bf16[2048,512]{1,0:T(8,128)(2,1)} %weights_hbm.1, bf16[64,16384]{1,0:T(8,128)(2,1)} %mentor_hbm.1, s32[16,128]{1,0:T(8,128)} %bitcast.2, s32[8]{0:T(128)} %lengths.1), custom_call_target="tpu_custom_call" | custom-call | tf_op jit(solution)/shard_map/pallas_call | solution.py:691
  114.1 0.6 copy.11
  114.7 1.3 %copy.12 = bf16[2048,512]{1,0:T(8,128)(2,1)} copy(bf16[2048,512]{1,0:T(8,128)(2,1)S(1)} %get-tuple-element.11) | data formatting | bytes 4194304

commit v8 on v7

--- a/solution.py
+++ b/solution.py
@@ -212,7 +212,7 @@
         return (
             stage(voc_buf, voc_sem, voc, NV, lambda i: at(dx=i // 2, dc=mod(i, 2))),
             stage(y_buf, y_sem, y, Y, lambda i: at(dy=i)),
-            stage(z_buf, z_sem, z, Z, lambda i: at(dz=i)),
+            stage(z_buf, z_sem, z, Z, lambda i: at(dz=turns(i - 1, Z))),
         )
 
     stat_stages = three(stat_voc, stat_y, stat_z, stat_voc_sem, stat_y_sem, stat_z_sem)

time: 118 us -> 118 us (level)
  no operation moved by 1% of the time
where the time goes in v8:
time: 118 us
  Pallas kernels  114 us (97%)
  between operations  2.33 us (2%)
  local copies, waits for them, and re-layouts  1.94 us (2%)
    pallas_call x1, Pallas kernels, body(): pl.pallas_call(functools.partial(kernel, dims), out_shape=(jax.ShapeDtype...  114 us

profile of v8, /device:TPU:1, one launch (start us, length us, event | category | flops | bytes accessed | tf_op | source)
XLA Modules:
  0.0 117.9 jit_solution(15036027971429261680)
XLA Ops:
  0.6 113.7 %shard_map.76 = (f32[1,1]{1,0:T(1,128)}, bf16[8,2048]{1,0:T(8,128)(2,1)S(1)}, bf16[2048,512]{1,0:T(8,128)(2,1)S(1)}) custom-call(bf16[64,2048]{1,0:T(8,128)(2,1)} %hidden.1, bf16[2048,512]{1,0:T(8,128)(2,1)} %weights_hbm.1, bf16[64,16384]{1,0:T(8,128)(2,1)} %mentor_hbm.1, s32[16,128]{1,0:T(8,128)} %bitcast.2, s32[8]{0:T(128)} %lengths.1), custom_call_target="tpu_custom_call" | custom-call | tf_op jit(solution)/shard_map/pallas_call | solution.py:691
  114.3 0.6 copy.11
  114.9 1.3 %copy.12 = bf16[2048,512]{1,0:T(8,128)(2,1)} copy(bf16[2048,512]{1,0:T(8,128)(2,1)S(1)} %get-tuple-element.11) | data formatting | bytes 4194304
